TPU v7x, 32 devices: a whole 2x2x4 slice. The times are simulated.
32 devices in a mesh: axial: 8 (over z, x), cross: 4 (over y, core).
Axes of the slice: x: 2, y: 2, z: 4, core: 2. Of those that a mesh axis runs over, the one named last changes fastest.
Arguments:
- cotangent: float32 [128, 32, 16, 128], P('axial', None, 'cross'), may hold values from -8 to 8
- diag_blocks: float32 [128, 32, 32], P('axial'), as said below
- lower_rates: float32 [128, 32], P('axial'), as said below
- upper_rates: float32 [128, 32], P('axial'), as said below
- cross_rate: float32 [32], replicated, may hold values from 0.02 to 0.24
- bin_profile: float32 [32], replicated, may hold values from 0.1 to 1
- open_cells: int32 [16, 128], replicated, may hold values 0 or 1
- segment_ids: int32 [128, 16], P('axial', 'cross'), may hold values from 0 to 127
Outputs:
- grad_state: float32 [128, 32, 16, 128], P('axial', None, 'cross')
- grad_emission: float32 [128], P(('axial', 'cross'))
Inputs may be any that keep to these rules, and one draw needn't show every extreme that they name: In every row (i, b) of the forward operator, diag_blocks[i, b, b] exceeds lower_rates[i, b] + upper_rates[i, b] + the sum of the magnitudes of the other entries of diag_blocks[i, b, :] by 1 or more. `lower_rates`: Positive. `upper_rates`: Positive.
All inputs are finite; a program needn't handle non-finite values.
Results may differ from a plain program's by a relative error of at most 0.0003.
Values sent between devices are 32-bit elements; how exact they have to be, the bound alone decides.
A program may use at most 64 MiB of HBM per device.

v0:
```python
import functools

import jax
import jax.numpy as jnp
from jax import lax
from jax.experimental import pallas as pl
from jax.experimental.pallas import tpu as pltpu
from jax.sharding import PartitionSpec as P

SEG_DEV = 4
PANEL_FEW = 8
PANEL_MANY = 4
MESH = pl.DeviceIdType.MESH
exact = lax.Precision.HIGHEST


def dot(a, b):
    return jnp.dot(a, b, precision=exact, preferred_element_type=jnp.float32)


def halves(x):
    high = x.astype(jnp.bfloat16)
    return high, (x - high.astype(jnp.float32)).astype(jnp.bfloat16)


def dot_split(a, b):
    (ah, al), (bh, bl) = a, halves(b)
    one = functools.partial(jnp.dot, preferred_element_type=jnp.float32)
    return one(ah, bh) + (one(ah, bl) + one(al, bh))


def invert(mats):
    size = mats[0].shape[0]
    panel = PANEL_FEW if len(mats) <= 4 else PANEL_MANY
    slabs = range(size // 8)
    row_id = lax.broadcasted_iota(jnp.int32, (8, size), 0)
    col_id = lax.broadcasted_iota(jnp.int32, (8, size), 1)
    mats = [[a[s * 8 : (s + 1) * 8] for s in slabs] for a in mats]
    for first in range(0, size, panel):
        spread = [
            [[jnp.broadcast_to(a[s][:, first + j : first + j + 1], (8, size)) for s in slabs] for j in range(panel)]
            for a in mats
        ]
        for j in range(panel):
            k = first + j
            home, at = k // 8, k % 8
            for i, a in enumerate(mats):
                col = spread[i][j]
                pivot = 1.0 / col[home][at : at + 1]
                row = jnp.where(col_id[:1] == k, 1.0, a[home][at : at + 1]) * pivot
                done = [jnp.where(col_id == k, 0.0, a[s]) - col[s] * row for s in slabs]
                done[home] = jnp.where(row_id == at, row, done[home])
                mats[i] = done
                for m in range(j + 1, panel):
                    other = spread[i][m]
                    entry = other[home][at : at + 1] * pivot
                    later = [other[s] - col[s] * entry for s in slabs]
                    later[home] = jnp.where(row_id == at, entry, later[home])
                    spread[i][m] = later
    return [jnp.concatenate(a, axis=0) for a in mats]


def kernel(n, nc, cot_hbm, diag_hbm, low_hbm, up_hbm, cross_hbm, prof_hbm, open_hbm, seg_hbm, out, out_seg, GH, GL,
           cot, diag, low, up, cross_rate, prof_rate, open_ref, seg, G, F, X, V, msg_out, msg_in, back_out, back_in,
           edge_out, edge_in, sum_out, sum_cross, sum_axial, s_in, s_msg, r_msg, s_back, r_back, s_hal, r_hal,
           s_edge, r_edge, s_cross, r_cross, s_axial, r_axial):
    pairs_in = [(cot_hbm, cot), (diag_hbm, diag), (low_hbm, low), (up_hbm, up), (cross_hbm, cross_rate), (prof_hbm, prof_rate),
                (open_hbm, open_ref), (seg_hbm, seg)]
    loads = [pltpu.make_async_copy(src, dst, s_in.at[i]) for i, (src, dst) in enumerate(pairs_in)]
    for i in (1, 0, 2, 3, 4, 5, 6, 7):
        loads[i].start()
    cells, nb = diag.shape[0], diag.shape[1]
    size = cells * nb
    rows = cot.shape[0] // size
    nz = cot.shape[1]
    per = rows * nz // n
    a = lax.axis_index("axial")
    c = lax.axis_index("cross")
    has_lo = c > 0
    has_hi = c < nc - 1

    barrier = pltpu.get_barrier_semaphore()
    for off in range(1, n):
        pl.semaphore_signal(barrier, inc=1, device_id=(lax.rem(a + off, n), c), device_id_type=MESH)

    for off in range(1, nc):
        pl.semaphore_signal(barrier, inc=1, device_id=(a, lax.rem(c + off, nc)), device_id_type=MESH)

    loads[1].wait()
    inverses = invert([diag[i] for i in range(cells)])

    loads[0].wait()
    for y in range(rows):
        F[:, (y + 1) * nz : (y + 2) * nz] = cot[pl.ds(y, size, stride=rows), :]

    pl.semaphore_wait(barrier, n - 1 + nc - 1)

    def hal_copy(down):
        src = F.at[:, nz : 2 * nz] if down else F.at[:, rows * nz : (rows + 1) * nz]
        dst = F.at[:, (rows + 1) * nz : (rows + 2) * nz] if down else F.at[:, 0:nz]
        way = 0 if down else 1
        return pltpu.make_async_remote_copy(
            src_ref=src, dst_ref=dst, send_sem=s_hal.at[way], recv_sem=r_hal.at[way],
            device_id=(a, c - 1 if down else c + 1), device_id_type=MESH)

    def edge_copy(down):
        way = 0 if down else 1
        return pltpu.make_async_remote_copy(
            src_ref=edge_out.at[way], dst_ref=edge_in.at[way], send_sem=s_edge.at[way], recv_sem=r_edge.at[way],
            device_id=(a, c - 1 if down else c + 1), device_id_type=MESH)

    @pl.when(has_lo)
    def _():
        hal_copy(True).start()

    @pl.when(has_hi)
    def _():
        hal_copy(False).start()

    @pl.when(jnp.logical_not(has_lo))
    def _():
        F[:, 0:nz] = jnp.zeros((size, nz), jnp.float32)

    @pl.when(jnp.logical_not(has_hi))
    def _():
        F[:, (rows + 1) * nz : (rows + 2) * nz] = jnp.zeros((size, nz), jnp.float32)

    for i in range(2, 8):
        loads[i].wait()
    V[...] = jnp.zeros(V.shape, jnp.float32)
    V[0:cells, 0:nb] = low[...]
    V[cells : 2 * cells, 0:nb] = up[...]
    V[2 * cells : 2 * cells + 1, 0:nb] = cross_rate[...]
    V[2 * cells + 1 : 2 * cells + 2, 0:nb] = prof_rate[...]
    V[2 * cells + 2 : 2 * cells + 2 + rows, 0:cells] = seg[...].astype(jnp.float32)
    V[...] = V[...].T
    low_col = [V[0:nb, j : j + 1] for j in range(cells)]
    up_col = [V[0:nb, cells + j : cells + j + 1] for j in range(cells)]
    cross_col = V[0:nb, 2 * cells : 2 * cells + 1]
    prof_col = V[0:nb, 2 * cells + 1 : 2 * cells + 2]
    seg_col = [V[0:cells, 2 * cells + 2 + y : 2 * cells + 3 + y] for y in range(rows)]

    eye = (lax.broadcasted_iota(jnp.int32, (nb, nb), 0) == lax.broadcasted_iota(jnp.int32, (nb, nb), 1)).astype(jnp.float32)

    G[...] = jnp.zeros(G.shape, jnp.float32)
    pack = 128 // nb
    same = (lax.broadcasted_iota(jnp.int32, (128, 128), 0) // nb) == (lax.broadcasted_iota(jnp.int32, (128, 128), 1) // nb)
    for g in range(cells // pack):
        tall = jnp.concatenate(inverses[g * pack : (g + 1) * pack], axis=0)
        wide = jnp.where(same, jnp.concatenate([tall] * pack, axis=1), 0.0)
        G[g * 128 : (g + 1) * 128, g * 128 : (g + 1) * 128] = wide.T
    chunk = 1
    while chunk < cells:
        width = chunk * nb
        joints = list(range(chunk, cells, 2 * chunk))
        parts, weights = [], []
        for j in joints:
            o, m = (j - chunk) * nb, j * nb
            lp = up_col[j - 1] * G[m - nb : m, m - nb : m]
            rq = low_col[j] * G[m : m + nb, m : m + nb]
            weights.append(eye - dot(rq, lp))
            parts.append((o, m, lp, rq))
        weights = invert(weights)
        for j, (o, m, lp, rq), w in zip(joints, parts, weights):
            span = max(128, 2 * width)
            lo = o // span * span
            row_l = up_col[j - 1] * G[m - nb : m, lo : lo + span]
            row_r = low_col[j] * G[m : m + nb, lo : lo + span]
            p = dot(w, row_r + dot(rq, row_l))
            q = row_l + dot(lp, p)
            col_l = G[o:m, m - nb : m]
            col_r = G[m : m + width, m : m + nb]
            G[o:m, lo : lo + span] += dot(col_l, p)
            G[m : m + width, lo : lo + span] += dot(col_r, q)
        chunk *= 2

    head, tail = low_col[0], up_col[cells - 1]
    g_head, g_tail = G[0:nb, :], G[size - nb : size, :]
    ends = jnp.concatenate([head * g_head, tail * g_tail], axis=0)
    field = dot(ends, F[:, nz : (rows + 1) * nz])
    ports = jnp.concatenate([ends[:, 0:nb], ends[:, size - nb : size]], axis=1)
    for e in range(n):
        bits = [ports, field[:, e * per : (e + 1) * per]]
        if 2 * nb + per < 128:
            bits.append(jnp.zeros((2 * nb, 128 - 2 * nb - per), jnp.float32))
        msg_out[e] = jnp.concatenate(bits, axis=1)

    def msg_copy(off):
        peer = lax.rem(a + off, n)
        return pltpu.make_async_remote_copy(
            src_ref=msg_out.at[peer], dst_ref=msg_in.at[a], send_sem=s_msg.at[off], recv_sem=r_msg.at[off],
            device_id=(peer, c), device_id_type=MESH)

    def back_copy(off):
        peer = lax.rem(a + off, n)
        return pltpu.make_async_remote_copy(
            src_ref=back_out.at[peer], dst_ref=back_in.at[a], send_sem=s_back.at[off], recv_sem=r_back.at[off],
            device_id=(peer, c), device_id_type=MESH)

    for off in range(1, n):
        msg_copy(off).start()
    msg_in[a] = msg_out[a]

    half = rows * nz // 2
    GH[...], GL[...] = halves(G[...])
    for part in range(2):
        at = slice(nz + part * half, nz + (part + 1) * half)
        X[:, at] = dot_split((GH[...], GL[...]), F[:, at])

    for off in range(1, n):
        msg_copy(off).wait_recv()

    lane = lax.broadcasted_iota(jnp.int32, (1, 128), 1)
    keep_l = jnp.where((lane >= nb) & (lane < 2 * nb), 0.0, 1.0)
    keep_r = jnp.where(lane < nb, 0.0, 1.0)
    groups = [(msg_in[d][0:nb], msg_in[d][nb : 2 * nb], None) for d in range(n)]
    while len(groups) > 1:
        pairs = [(groups[i], groups[i + 1]) for i in range(0, len(groups), 2)]
        weights = invert([eye - dot(r[0][:, 0:nb], l[1][:, nb : 2 * nb]) for l, r in pairs])
        top = len(pairs) == 1
        groups = []
        for (l, r), w in zip(pairs, weights):
            from_l, from_r = l[1] * keep_l, r[0] * keep_r
            p = dot(w, from_r + dot(r[0][:, 0:nb], from_l))
            q = from_l + dot(l[1][:, nb : 2 * nb], p)
            left = l[0] if l[2] is None else jnp.concatenate([l[0], l[2]], axis=0)
            right = r[1] if r[2] is None else jnp.concatenate([r[1], r[2]], axis=0)
            left = left * keep_l + dot(left[:, nb : 2 * nb], p)
            right = right * keep_r + dot(right[:, 0:nb], q)
            inner = [p, q]
            if l[2] is not None:
                inner = [left[nb:]] + inner
            if r[2] is not None:
                inner = inner + [right[nb:]]
            groups.append((left[0:nb], right[0:nb], jnp.concatenate(inner, axis=0)))
    inner = groups[0][2]
    none = jnp.zeros((nb, 128), jnp.float32)
    for d in range(n):
        if d == 0:
            back_out[d] = jnp.concatenate([none, inner[0:nb]], axis=0)
        elif d == n - 1:
            back_out[d] = jnp.concatenate([inner[(2 * d - 1) * nb :], none], axis=0)
        else:
            back_out[d] = inner[(2 * d - 1) * nb : (2 * d + 1) * nb]
    for off in range(1, n):
        back_copy(off).start()
    back_in[a] = back_out[a]

    @pl.when(has_lo)
    def _():
        hal_copy(True).wait_send()
        hal_copy(False).wait_recv()

    @pl.when(has_hi)
    def _():
        hal_copy(False).wait_send()
        hal_copy(True).wait_recv()

    sides = dot_split((GH[...], GL[...]), jnp.concatenate([F[:, 0:nz], F[:, (rows + 1) * nz : (rows + 2) * nz]], axis=1))
    X[:, 0:nz] = sides[:, 0:nz]
    X[:, (rows + 1) * nz : (rows + 2) * nz] = sides[:, nz : 2 * nz]

    for off in range(1, n):
        back_copy(off).wait_recv()

    each = n // rows
    flux = []
    for y in range(rows):
        flux.append(jnp.concatenate([back_in[y * each + e][:, 2 * nb : 2 * nb + per] for e in range(each)], axis=1))
    edge_out[0] = flux[0]
    edge_out[1] = flux[rows - 1]

    @pl.when(has_lo)
    def _():
        edge_copy(True).start()

    @pl.when(has_hi)
    def _():
        edge_copy(False).start()

    gc = (jnp.concatenate([GH[:, 0:nb], GH[:, size - nb : size]], axis=1),
          jnp.concatenate([GL[:, 0:nb], GL[:, size - nb : size]], axis=1))
    X[:, nz : (rows + 1) * nz] += dot_split(gc, jnp.concatenate(flux, axis=1))

    opens = []
    for y in range(-1, rows + 1):
        at = jnp.clip(c * rows + y, 0, nc * rows - 1)
        line = open_ref[pl.ds(at, 1), :].astype(jnp.float32)
        if y == -1:
            line = jnp.where(has_lo, line, 0.0)
        if y == rows:
            line = jnp.where(has_hi, line, 0.0)
        opens.append(line)

    segs = sum_out.shape[-1]
    seg_id = lax.broadcasted_iota(jnp.int32, (1, segs), 1)
    gain = jnp.zeros((8, segs), jnp.float32)
    for y in range(rows):
        bits = []
        for i in range(cells):
            sent = X[i * nb : (i + 1) * nb, (y + 1) * nz : (y + 2) * nz] * prof_col
            bits.append(jnp.sum(sent, axis=0, keepdims=True))
        given = jnp.sum(jnp.concatenate(bits, axis=0) * opens[y + 1], axis=1, keepdims=True) * (1.0 / nz)
        picked = jnp.where(seg_col[y] == seg_id.astype(jnp.float32), given, 0.0)
        for i in range(cells // 8):
            gain = gain + picked[i * 8 : (i + 1) * 8]
    sum_out[0] = gain

    def cross_copy(off):
        return pltpu.make_async_remote_copy(
            src_ref=sum_out.at[0], dst_ref=sum_cross.at[off], send_sem=s_cross.at[off], recv_sem=r_cross.at[off],
            device_id=(a, lax.rem(c + off, nc)), device_id_type=MESH)

    def axial_copy(off):
        return pltpu.make_async_remote_copy(
            src_ref=sum_out.at[1], dst_ref=sum_axial.at[off], send_sem=s_axial.at[off], recv_sem=r_axial.at[off],
            device_id=(lax.rem(a + off, n), c), device_id_type=MESH)

    for off in range(1, nc):
        cross_copy(off).start()

    zlane = lax.broadcasted_iota(jnp.int32, (1, nz), 1)
    step_col = jnp.concatenate([cross_col] * 4, axis=0)
    block = 4 * nb
    for y in list(range(1, rows - 1)) + [0, rows - 1]:
        if y == 0:
                @pl.when(has_lo)
                def _():
                    edge_copy(True).wait_send()
                    edge_copy(False).wait_recv()
                    X[:, 0:nz] += dot_split(gc, edge_in[1])

                @pl.when(has_hi)
                def _():
                    edge_copy(False).wait_send()
                    edge_copy(True).wait_recv()
                    X[:, (rows + 1) * nz : (rows + 2) * nz] += dot_split(gc, edge_in[0])

        here = opens[y + 1]
        before = jnp.where(zlane == 0, 0.0, pltpu.roll(here, 1, 1)) * here
        after = jnp.where(zlane == nz - 1, 0.0, pltpu.roll(here, nz - 1, 1)) * here
        above = opens[y] * here
        below = opens[y + 2] * here
        total = before + after + above + below
        for i in range(size // block):
            at = slice(i * block, (i + 1) * block)
            x = X[at, (y + 1) * nz : (y + 2) * nz]
            moved = (above * (X[at, y * nz : (y + 1) * nz] - x) + below * (X[at, (y + 2) * nz : (y + 3) * nz] - x)
                     + before * (pltpu.roll(x, 1, 1) - x) + after * (pltpu.roll(x, nz - 1, 1) - x))
            out[pl.ds(i * block * rows + y, block, stride=rows), :] = x + step_col * moved
        if y == 1:
            gain = sum_out[0]
            for off in range(1, nc):
                cross_copy(off).wait_recv()
                gain = gain + sum_cross[off]
            sum_out[1] = gain
            for off in range(1, n):
                axial_copy(off).start()

    gain = sum_out[1]
    for off in range(1, n):
        axial_copy(off).wait_recv()
        gain = gain + sum_axial[off]
    gain = jnp.sum(gain, axis=0, keepdims=True)
    own = out_seg.shape[1]
    own_id = lax.broadcasted_iota(jnp.int32, (1, own), 1)
    result = jnp.zeros((1, own), jnp.float32)
    for j in range(own):
        mine = jnp.sum(jnp.where(seg_id == (a * nc + c) * own + j, gain, 0.0), axis=1, keepdims=True)
        result = jnp.where(own_id == j, mine, result)
    out_seg[...] = result

    for off in range(1, nc):
        cross_copy(off).wait_send()
    for off in range(1, n):
        axial_copy(off).wait_send()

    for off in range(1, n):
        msg_copy(off).wait_send()
        back_copy(off).wait_send()


def per_device(n, nc, cotangent, diag_blocks, lower_rates, upper_rates, cross_rate, bin_profile, open_cells, segment_ids):
    cells, nb, rows, nz = cotangent.shape
    size = cells * nb
    segs = SEG_DEV * n * nc
    vmem = pl.BlockSpec(memory_space=pltpu.VMEM)
    hbm = pl.BlockSpec(memory_space=pltpu.HBM)
    dma = pltpu.SemaphoreType.DMA
    f32 = jnp.float32
    operands = (
        cotangent.reshape(size * rows, nz), diag_blocks, lower_rates, upper_rates,
        cross_rate.reshape(1, nb), bin_profile.reshape(1, nb), open_cells, segment_ids.T,
    )
    grad, gain = pl.pallas_call(
        functools.partial(kernel, n, nc),
        out_shape=(jax.ShapeDtypeStruct((size * rows, nz), f32), jax.ShapeDtypeStruct((1, SEG_DEV), f32)),
        in_specs=[hbm] * len(operands),
        out_specs=(vmem, vmem),
        scratch_shapes=[pltpu.VMEM((size, size), jnp.bfloat16)] * 2 + [pltpu.VMEM(x.shape, x.dtype) for x in operands] + [
            pltpu.VMEM((size, size), f32),
            pltpu.VMEM((size, (rows + 2) * nz), f32),
            pltpu.VMEM((size, (rows + 2) * nz), f32),
            pltpu.VMEM((128, 128), f32),
            pltpu.VMEM((n, 2 * nb, 128), f32),
            pltpu.VMEM((n, 2 * nb, 128), f32),
            pltpu.VMEM((n, 2 * nb, 128), f32),
            pltpu.VMEM((n, 2 * nb, 128), f32),
            pltpu.VMEM((2, 2 * nb, nz), f32),
            pltpu.VMEM((2, 2 * nb, nz), f32),
            pltpu.VMEM((2, 8, segs), f32),
            pltpu.VMEM((nc, 8, segs), f32),
            pltpu.VMEM((n, 8, segs), f32),
            dma((len(operands),)), dma((n,)), dma((n,)), dma((n,)), dma((n,)), dma((2,)), dma((2,)), dma((2,)), dma((2,)),
            dma((nc,)), dma((nc,)), dma((n,)), dma((n,)),
        ],
        compiler_params=pltpu.CompilerParams(
            collective_id=0, has_side_effects=True, vmem_limit_bytes=63 * 1024 * 1024 + 512 * 1024
        ),
    )(*operands)
    return grad.reshape(cotangent.shape), gain.reshape(SEG_DEV)


def solution(mesh):
    in_specs = (
        P("axial", None, "cross", None),
        P("axial", None, None),
        P("axial", None),
        P("axial", None),
        P(),
        P(),
        P(),
        P("axial", "cross"),
    )
    out_specs = (P("axial", None, "cross", None), P(("axial", "cross")))
    return jax.shard_map(
        functools.partial(per_device, mesh.shape["axial"], mesh.shape["cross"]),
        mesh=mesh, in_specs=in_specs, out_specs=out_specs, check_vma=False,
    )
```

profile of v0, /device:TPU:0, one launch (start us, length us, event | category | flops | bytes accessed | tf_op | source)
XLA Modules:
  0.0 55.5 jit_solution(7335909509998957214)
XLA Ops:
  0.6 52.0 %shard_map.95 = (f32[2048,128]{1,0:T(8,128)}, f32[1,4]{1,0:T(1,128)}) custom-call(f32[2048,128]{1,0:T(8,128)} %bitcast.6, f32[16,32,32]{2,1,0:T(8,128)} %diag_hbm.1, f32[16,32]{1,0:T(8,128)} %low_hbm.1, f32[16,32]{1,0:T(8,128)} %up_hbm.1, f32[1,32]{1,0:T(1,128)} %bitcast.9, f32[1,32]{1,0:T(1,128)} %bitcast.10, s32[16,128]{1,0:T(8,128)} %open_hbm.1, ...), custom_call_target="tpu_custom_call" | custom-call | tf_op jit(solution)/shard_map/pallas_call | solution.py:395
  52.6 0.0 copy-start
  52.7 2.3 %copy.12 = f32[16,32,4,128]{3,2,1,0:T(4,128)} copy(f32[16,32,4,128]{3,2,1,0:T(4,128)} %bitcast.7) | data formatting | bytes 2097152
  55.0 0.0 copy-done
  55.0 0.5 copy.13
Async XLA Ops:
  52.6 2.3 %copy-start = (f32[1,4]{1,0:T(1,128)S(1)}, f32[1,4]{1,0:T(1,128)}, u32[]{:S(2)}) copy-start(f32[1,4]{1,0:T(1,128)} %get-tuple-element.5) | copy-start | bytes 52
where the time goes:
time: 55.6 us; the launch traced here: 55.5 us
  Pallas kernels  52 us (94%)
  local copies, waits for them, and re-layouts  2.81 us (5%)
  between operations  0.65 us (1%)
    pallas_call x1, Pallas kernels, per_device(): pl.pallas_call(functools.partial(kernel, n, nc), out_shape=(jax.ShapeDtyp...  52 us
    unnamed x4, local copies, waits for them, and re-layouts  2.81 us

commit v1 on v0

v1 whole, which is shorter than its diff:
```python
import functools

import jax
import jax.numpy as jnp
from jax import lax
from jax.experimental import pallas as pl
from jax.experimental.pallas import tpu as pltpu
from jax.sharding import PartitionSpec as P

SEG_DEV = 4
MESH = pl.DeviceIdType.MESH
exact = lax.Precision.HIGHEST


def dot(a, b):
    return jnp.dot(a, b, precision=exact, preferred_element_type=jnp.float32)


def halves(x):
    high = x.astype(jnp.bfloat16)
    return high, (x - high.astype(jnp.float32)).astype(jnp.bfloat16)


def dot_halves(a, b):
    (ah, al), (bh, bl) = a, b
    one = functools.partial(jnp.dot, preferred_element_type=jnp.float32)
    return one(ah, bh) + (one(ah, bl) + one(al, bh))


def dot_split(a, b):
    return dot_halves(a, halves(b))


def dot3(a, b):
    return dot_halves(halves(a), halves(b))


def dot_split_b(a, b):
    return dot_halves(halves(a), b)


def spread(x, k, nb):
    packs, height, width = x.shape
    flat = x.reshape(packs * height, width)
    lane = lax.broadcasted_iota(jnp.int32, flat.shape, 1)
    return jnp.take_along_axis(flat, lane // nb * nb + k, axis=1).reshape(x.shape)


def invert_packs(a, nb):
    packs, _, width = a.shape
    row_id = lax.broadcasted_iota(jnp.int32, (packs, 8, width), 1)
    for first in range(0, nb, 8):
        home = a[:, first : first + 8]
        rest = [x for x in (a[:, :first], a[:, first + 8 :]) if x.shape[1]]
        rest = jnp.concatenate(rest, axis=1) if len(rest) > 1 else rest[0]
        near = [spread(home, first + j, nb) for j in range(8)]
        far = [spread(rest, first + j, nb) for j in range(8)]
        at = lax.broadcasted_iota(jnp.int32, home.shape, 2) % nb - first
        home = jnp.where((at >= 0) & (at < 8), jnp.where(at == row_id, 1.0, 0.0), home)
        at = lax.broadcasted_iota(jnp.int32, rest.shape, 2) % nb - first
        rest = jnp.where((at >= 0) & (at < 8), 0.0, rest)
        for j in range(8):
            pivot = 1.0 / jnp.broadcast_to(near[j][:, j : j + 1], home.shape)
            row = jnp.broadcast_to(home[:, j : j + 1], home.shape) * pivot
            home = jnp.where(row_id == j, row, home - near[j] * row)
            for m in range(j + 1, 8):
                entry = jnp.broadcast_to(near[m][:, j : j + 1], home.shape) * pivot
                near[m] = jnp.where(row_id == j, entry, near[m] - near[j] * entry)
        for j in range(8):
            rest = rest - far[j] * home[:, j : j + 1]
        a = jnp.concatenate([x for x in (rest[:, :first], home, rest[:, first:]) if x.shape[1]], axis=1)
    return a


def invert(mats):
    nb = mats[0].shape[0]
    pack = 128 // nb
    padded = list(mats)
    while len(padded) % pack:
        padded.append(mats[len(padded) % len(mats)])
    packs = [jnp.concatenate(padded[i : i + pack], axis=1) for i in range(0, len(padded), pack)]
    done = invert_packs(jnp.stack(packs), nb)
    return [done[i // pack, :, i % pack * nb : (i % pack + 1) * nb] for i in range(len(mats))]


def kernel(n, nc, cot_hbm, diag_hbm, low_hbm, up_hbm, cross_hbm, prof_hbm, open_hbm, seg_hbm, out, out_seg, GH, GL, FH, FL,
           cot, diag, low, up, cross_rate, prof_rate, open_ref, seg, G, F, X, V, port_out, port_in, msg_out, msg_in, back_out, back_in,
           edge_out, edge_in, sum_out, sum_cross, sum_axial, s_in, s_port, r_port, s_msg, r_msg, s_back, r_back, s_hal, r_hal,
           s_edge, r_edge, s_cross, r_cross, s_axial, r_axial):
    pairs_in = [(cot_hbm, cot), (diag_hbm, diag), (low_hbm, low), (up_hbm, up), (cross_hbm, cross_rate), (prof_hbm, prof_rate),
                (open_hbm, open_ref), (seg_hbm, seg)]
    loads = [pltpu.make_async_copy(src, dst, s_in.at[i]) for i, (src, dst) in enumerate(pairs_in)]
    for i in (1, 0, 2, 3, 4, 5, 6, 7):
        loads[i].start()
    cells, nb = diag.shape[0], diag.shape[1]
    size = cells * nb
    rows = cot.shape[0] // size
    nz = cot.shape[1]
    per = rows * nz // n
    a = lax.axis_index("axial")
    c = lax.axis_index("cross")
    has_lo = c > 0
    has_hi = c < nc - 1

    barrier = pltpu.get_barrier_semaphore()
    for off in range(1, n):
        pl.semaphore_signal(barrier, inc=1, device_id=(lax.rem(a + off, n), c), device_id_type=MESH)

    for off in range(1, nc):
        pl.semaphore_signal(barrier, inc=1, device_id=(a, lax.rem(c + off, nc)), device_id_type=MESH)

    for i in range(2, 8):
        loads[i].wait()
    V[...] = jnp.zeros(V.shape, jnp.float32)
    V[0:cells, 0:nb] = low[...]
    V[cells : 2 * cells, 0:nb] = up[...]
    V[2 * cells : 2 * cells + 1, 0:nb] = cross_rate[...]
    V[2 * cells + 2 : 2 * cells + 2 + rows, 0:cells] = seg[...].astype(jnp.float32)
    V[...] = V[...].T
    low_col = [V[0:nb, j : j + 1] for j in range(cells)]
    up_col = [V[0:nb, cells + j : cells + j + 1] for j in range(cells)]
    cross_col = V[0:nb, 2 * cells : 2 * cells + 1]
    seg_col = [V[0:cells, 2 * cells + 2 + y : 2 * cells + 3 + y] for y in range(rows)]
    eye = (lax.broadcasted_iota(jnp.int32, (nb, nb), 0) == lax.broadcasted_iota(jnp.int32, (nb, nb), 1)).astype(jnp.float32)

    loads[1].wait()
    pack = 128 // nb
    inverses = invert_packs(
        jnp.stack([jnp.concatenate([diag[g * pack + i] for i in range(pack)], axis=1) for g in range(cells // pack)]), nb)
    tall = [inverses[g].T for g in range(cells // pack)]

    loads[0].wait()
    for y in range(rows):
        F[:, (y + 1) * nz : (y + 2) * nz] = cot[pl.ds(y, size, stride=rows), :]
    main = slice(nz, (rows + 1) * nz)

    pl.semaphore_wait(barrier, n - 1 + nc - 1)

    def hal_copy(down):
        src = F.at[:, nz : 2 * nz] if down else F.at[:, rows * nz : (rows + 1) * nz]
        dst = F.at[:, (rows + 1) * nz : (rows + 2) * nz] if down else F.at[:, 0:nz]
        way = 0 if down else 1
        return pltpu.make_async_remote_copy(
            src_ref=src, dst_ref=dst, send_sem=s_hal.at[way], recv_sem=r_hal.at[way],
            device_id=(a, c - 1 if down else c + 1), device_id_type=MESH)

    def edge_copy(down):
        way = 0 if down else 1
        return pltpu.make_async_remote_copy(
            src_ref=edge_out.at[way], dst_ref=edge_in.at[way], send_sem=s_edge.at[way], recv_sem=r_edge.at[way],
            device_id=(a, c - 1 if down else c + 1), device_id_type=MESH)

    @pl.when(has_lo)
    def _():
        hal_copy(True).start()

    @pl.when(has_hi)
    def _():
        hal_copy(False).start()

    @pl.when(jnp.logical_not(has_lo))
    def _():
        F[:, 0:nz] = jnp.zeros((size, nz), jnp.float32)

    @pl.when(jnp.logical_not(has_hi))
    def _():
        F[:, (rows + 1) * nz : (rows + 2) * nz] = jnp.zeros((size, nz), jnp.float32)

    FH[:, main], FL[:, main] = halves(F[:, main])

    groups = []
    for i in range(cells):
        one = tall[i // pack][i % pack * nb : (i % pack + 1) * nb]
        groups.append(jnp.concatenate([low_col[i] * one, up_col[i] * one], axis=0))
    levels = []
    while len(groups) > 1:
        pairs = [(groups[i], groups[i + 1]) for i in range(0, len(groups), 2)]
        width = groups[0].shape[1]
        none = jnp.zeros((nb, width), jnp.float32)
        meets = [dot(r[:, 0:nb], l[nb:]) for l, r in pairs]
        weights = invert([eye - k[:nb, width - nb :] for k in meets])
        level = []
        groups = []
        for (l, r), k, w in zip(pairs, meets, weights):
            p = dot(w, jnp.concatenate([k[:nb], r[:nb]], axis=1))
            base = jnp.concatenate([jnp.concatenate([l[:nb], none], axis=1), jnp.concatenate([k[nb:], r[nb:]], axis=1)], axis=0)
            groups.append(base + dot(jnp.concatenate([l[:nb, width - nb :], k[nb:, width - nb :]], axis=0), p))
            level.append(p)
        levels.append(level)

    ends = groups[0]
    ports = jnp.concatenate([ends[:, 0:nb], ends[:, size - nb : size]], axis=1)
    port_out[...] = jnp.concatenate([ports[:nb], ports[nb:]], axis=1)

    def port_copy(off):
        peer = lax.rem(a + off, n)
        return pltpu.make_async_remote_copy(
            src_ref=port_out, dst_ref=port_in.at[a], send_sem=s_port.at[off], recv_sem=r_port.at[off],
            device_id=(peer, c), device_id_type=MESH)

    def msg_copy(off):
        peer = lax.rem(a + off, n)
        return pltpu.make_async_remote_copy(
            src_ref=msg_out.at[peer], dst_ref=msg_in.at[a], send_sem=s_msg.at[off], recv_sem=r_msg.at[off],
            device_id=(peer, c), device_id_type=MESH)

    def back_copy(off):
        peer = lax.rem(a + off, n)
        return pltpu.make_async_remote_copy(
            src_ref=back_out.at[peer], dst_ref=back_in.at[a], send_sem=s_back.at[off], recv_sem=r_back.at[off],
            device_id=(peer, c), device_id_type=MESH)

    for off in range(1, n):
        port_copy(off).start()
    port_in[a] = port_out[...]
    field = dot_split_b(ends, (FH[:, main], FL[:, main]))
    for e in range(n):
        bits = [field[:nb, e * per : (e + 1) * per], field[nb:, e * per : (e + 1) * per]]
        if per < 64:
            blank = jnp.zeros((nb, 64 - per), jnp.float32)
            bits = [bits[0], blank, bits[1], blank]
        msg_out[e] = jnp.concatenate(bits, axis=1)
    for off in range(1, n):
        msg_copy(off).start()
    msg_in[a] = msg_out[a]

    G[...] = jnp.zeros(G.shape, jnp.float32)
    same = (lax.broadcasted_iota(jnp.int32, (128, 128), 0) // nb) == (lax.broadcasted_iota(jnp.int32, (128, 128), 1) // nb)
    for g in range(cells // pack):
        G[g * 128 : (g + 1) * 128, g * 128 : (g + 1) * 128] = jnp.where(same, jnp.concatenate([tall[g]] * pack, axis=1), 0.0)
    width = nb
    for level in levels:
        span = max(128, 2 * width)
        for i, p in enumerate(level):
            o, m = 2 * i * width, (2 * i + 1) * width
            lo = o // span * span
            if span > 2 * width:
                blank = [jnp.zeros((nb, x), jnp.float32) for x in (o - lo, lo + span - o - 2 * width)]
                p = jnp.concatenate([x for x in (blank[0], p, blank[1]) if x.shape[1]], axis=1)
            left = G[o:m, lo : lo + span] + dot3(G[o:m, m - nb : m], p)
            G[m : m + width, lo : lo + span] += dot3(G[m : m + width, m : m + nb], up_col[m // nb - 1] * left[width - nb :])
            G[o:m, lo : lo + span] = left
        width *= 2

    half = rows * nz // 2
    GH[...], GL[...] = halves(G[...])
    for part in range(2):
        at = slice(nz + part * half, nz + (part + 1) * half)
        X[:, at] = dot_halves((GH[...], GL[...]), (FH[:, at], FL[:, at]))

    for off in range(1, n):
        port_copy(off).wait_recv()

    lane = lax.broadcasted_iota(jnp.int32, (1, 128), 1)
    keep_l = jnp.where((lane >= nb) & (lane < 2 * nb), 0.0, 1.0)
    keep_r = jnp.where(lane < nb, 0.0, 1.0)
    field_in = None
    groups = [(port_in[d][:, 0 : 2 * nb], port_in[d][:, 2 * nb :], None) for d in range(n)]
    while len(groups) > 1:
        pairs = [(groups[i], groups[i + 1]) for i in range(0, len(groups), 2)]
        meets = [dot(r[0][:, 0:nb], l[1][:, nb : 2 * nb]) for l, r in pairs]
        weights = invert([eye - k for k in meets])
        if field_in is None:
            for off in range(1, n):
                msg_copy(off).wait_recv()
            field_in = [msg_in[d] for d in range(n)]
            groups = [(jnp.concatenate([f[:, 0 : 2 * nb], h[:, 0:64]], axis=1), jnp.concatenate([t, h[:, 64:]], axis=1), None)
                      for (f, t, _), h in zip(groups, field_in)]
            pairs = [(groups[i], groups[i + 1]) for i in range(0, len(groups), 2)]
        rights = [jnp.concatenate(r[0:2] if r[2] is None else r, axis=0) for l, r in pairs]
        meets = [dot(r[:, 0:nb], l[1]) for (l, _), r in zip(pairs, rights)]
        groups = []
        for (l, _), r, k, w in zip(pairs, rights, meets, weights):
            p = dot(w, k[:nb] * keep_l + r[:nb] * keep_r)
            left = jnp.concatenate([l[0], l[1]] if l[2] is None else [l[0], l[2], l[1]], axis=0)
            base = jnp.concatenate([left * keep_l, k[nb:] * keep_l + r[nb:] * keep_r], axis=0)
            both = base + dot(jnp.concatenate([left[:, nb : 2 * nb], k[nb:, nb : 2 * nb]], axis=0), p)
            seam = left.shape[0]
            inner = [both[nb : seam - nb], p, both[seam - nb : seam], both[seam + nb :]]
            groups.append((both[:nb], both[seam : seam + nb], jnp.concatenate([x for x in inner if x.shape[0]], axis=0)))
    inner = groups[0][2]
    none = jnp.zeros((nb, 64), jnp.float32)
    for d in range(n):
        sides = [inner[(2 * d - 1) * nb : 2 * d * nb, 2 * nb :] if d > 0 else none,
                 inner[2 * d * nb : (2 * d + 1) * nb, 2 * nb :] if d < n - 1 else none]
        back_out[d] = jnp.concatenate(sides, axis=1)
    for off in range(1, n):
        back_copy(off).start()
    back_in[a] = back_out[a]

    @pl.when(has_lo)
    def _():
        hal_copy(True).wait_send()
        hal_copy(False).wait_recv()

    @pl.when(has_hi)
    def _():
        hal_copy(False).wait_send()
        hal_copy(True).wait_recv()

    sides = dot_split((GH[...], GL[...]), jnp.concatenate([F[:, 0:nz], F[:, (rows + 1) * nz : (rows + 2) * nz]], axis=1))
    X[:, 0:nz] = sides[:, 0:nz]
    X[:, (rows + 1) * nz : (rows + 2) * nz] = sides[:, nz : 2 * nz]

    sent = jnp.concatenate([prof_rate[...]] * cells, axis=1)
    mine = lax.broadcasted_iota(jnp.int32, (cells, size), 1) // nb == lax.broadcasted_iota(jnp.int32, (cells, size), 0)
    sent = dot_halves(halves(jnp.where(mine, sent, 0.0)), (GH[...], GL[...]))
    emit = dot_split_b(sent, (FH[:, main], FL[:, main]))
    sent = jnp.concatenate([sent[:, 0:nb], sent[:, size - nb : size]], axis=1)

    for off in range(1, n):
        back_copy(off).wait_recv()

    each = n // rows
    flux = []
    for y in range(rows):
        flux.append(jnp.concatenate([
            jnp.concatenate([back_in[y * each + e][:, at : at + per] for e in range(each)], axis=1) for at in (0, 64)], axis=0))
    edge_out[0] = flux[0]
    edge_out[1] = flux[rows - 1]

    @pl.when(has_lo)
    def _():
        edge_copy(True).start()

    @pl.when(has_hi)
    def _():
        edge_copy(False).start()

    opens = []
    for y in range(-1, rows + 1):
        at = jnp.clip(c * rows + y, 0, nc * rows - 1)
        line = open_ref[pl.ds(at, 1), :].astype(jnp.float32)
        if y == -1:
            line = jnp.where(has_lo, line, 0.0)
        if y == rows:
            line = jnp.where(has_hi, line, 0.0)
        opens.append(line)

    segs = sum_out.shape[-1]
    seg_id = lax.broadcasted_iota(jnp.int32, (1, segs), 1)
    gain = jnp.zeros((8, segs), jnp.float32)
    flux = halves(jnp.concatenate(flux, axis=1))
    emit = emit + dot_halves(halves(sent), flux)
    for y in range(rows):
        given = jnp.sum(emit[:, y * nz : (y + 1) * nz] * opens[y + 1], axis=1, keepdims=True) * (1.0 / nz)
        picked = jnp.where(seg_col[y] == seg_id.astype(jnp.float32), given, 0.0)
        for i in range(cells // 8):
            gain = gain + picked[i * 8 : (i + 1) * 8]
    sum_out[0] = gain

    def cross_copy(off):
        return pltpu.make_async_remote_copy(
            src_ref=sum_out.at[0], dst_ref=sum_cross.at[off], send_sem=s_cross.at[off], recv_sem=r_cross.at[off],
            device_id=(a, lax.rem(c + off, nc)), device_id_type=MESH)

    def axial_copy(off):
        return pltpu.make_async_remote_copy(
            src_ref=sum_out.at[1], dst_ref=sum_axial.at[off], send_sem=s_axial.at[off], recv_sem=r_axial.at[off],
            device_id=(lax.rem(a + off, n), c), device_id_type=MESH)

    for off in range(1, nc):
        cross_copy(off).start()

    gc = (jnp.concatenate([GH[:, 0:nb], GH[:, size - nb : size]], axis=1),
          jnp.concatenate([GL[:, 0:nb], GL[:, size - nb : size]], axis=1))
    X[:, main] += dot_halves(gc, flux)

    zlane = lax.broadcasted_iota(jnp.int32, (1, nz), 1)
    step_col = jnp.concatenate([cross_col] * 4, axis=0)
    block = 4 * nb
    for y in list(range(1, rows - 1)) + [0, rows - 1]:
        if y == 0:
                @pl.when(has_lo)
                def _():
                    edge_copy(True).wait_send()
                    edge_copy(False).wait_recv()
                    X[:, 0:nz] += dot_split(gc, edge_in[1])

                @pl.when(has_hi)
                def _():
                    edge_copy(False).wait_send()
                    edge_copy(True).wait_recv()
                    X[:, (rows + 1) * nz : (rows + 2) * nz] += dot_split(gc, edge_in[0])

        here = opens[y + 1]
        before = jnp.where(zlane == 0, 0.0, pltpu.roll(here, 1, 1)) * here
        after = jnp.where(zlane == nz - 1, 0.0, pltpu.roll(here, nz - 1, 1)) * here
        above = opens[y] * here
        below = opens[y + 2] * here
        total = before + after + above + below
        for i in range(size // block):
            at = slice(i * block, (i + 1) * block)
            x = X[at, (y + 1) * nz : (y + 2) * nz]
            moved = (above * (X[at, y * nz : (y + 1) * nz] - x) + below * (X[at, (y + 2) * nz : (y + 3) * nz] - x)
                     + before * (pltpu.roll(x, 1, 1) - x) + after * (pltpu.roll(x, nz - 1, 1) - x))
            out[pl.ds(i * block * rows + y, block, stride=rows), :] = x + step_col * moved
        if y == 1:
            gain = sum_out[0]
            for off in range(1, nc):
                cross_copy(off).wait_recv()
                gain = gain + sum_cross[off]
            sum_out[1] = gain
            for off in range(1, n):
                axial_copy(off).start()

    gain = sum_out[1]
    for off in range(1, n):
        axial_copy(off).wait_recv()
        gain = gain + sum_axial[off]
    gain = jnp.sum(gain, axis=0, keepdims=True)
    own = out_seg.shape[1]
    own_id = lax.broadcasted_iota(jnp.int32, (1, own), 1)
    result = jnp.zeros((1, own), jnp.float32)
    for j in range(own):
        mine = jnp.sum(jnp.where(seg_id == (a * nc + c) * own + j, gain, 0.0), axis=1, keepdims=True)
        result = jnp.where(own_id == j, mine, result)
    out_seg[...] = result

    for off in range(1, nc):
        cross_copy(off).wait_send()
    for off in range(1, n):
        axial_copy(off).wait_send()

    for off in range(1, n):
        port_copy(off).wait_send()
        msg_copy(off).wait_send()
        back_copy(off).wait_send()


def per_device(n, nc, cotangent, diag_blocks, lower_rates, upper_rates, cross_rate, bin_profile, open_cells, segment_ids):
    cells, nb, rows, nz = cotangent.shape
    size = cells * nb
    segs = SEG_DEV * n * nc
    vmem = pl.BlockSpec(memory_space=pltpu.VMEM)
    hbm = pl.BlockSpec(memory_space=pltpu.HBM)
    dma = pltpu.SemaphoreType.DMA
    f32 = jnp.float32
    operands = (
        cotangent.reshape(size * rows, nz), diag_blocks, lower_rates, upper_rates,
        cross_rate.reshape(1, nb), bin_profile.reshape(1, nb), open_cells, segment_ids.T,
    )
    operands = [pltpu.with_memory_space_constraint(x, pltpu.HBM) for x in operands]
    grad, gain = pl.pallas_call(
        functools.partial(kernel, n, nc),
        out_shape=(pltpu.VMEM((size * rows, nz), f32), jax.ShapeDtypeStruct((1, SEG_DEV), f32)),
        in_specs=[hbm] * len(operands),
        out_specs=(vmem, vmem),
        scratch_shapes=[pltpu.VMEM((size, size), jnp.bfloat16)] * 2 + [pltpu.VMEM((size, rows * nz + 2 * nz), jnp.bfloat16)] * 2 + [pltpu.VMEM(x.shape, x.dtype) for x in operands] + [
            pltpu.VMEM((size, size), f32),
            pltpu.VMEM((size, (rows + 2) * nz), f32),
            pltpu.VMEM((size, (rows + 2) * nz), f32),
            pltpu.VMEM((128, 128), f32),
            pltpu.VMEM((nb, 128), f32),
            pltpu.VMEM((n, nb, 128), f32),
            pltpu.VMEM((n, nb, 128), f32),
            pltpu.VMEM((n, nb, 128), f32),
            pltpu.VMEM((n, nb, 128), f32),
            pltpu.VMEM((n, nb, 128), f32),
            pltpu.VMEM((2, 2 * nb, nz), f32),
            pltpu.VMEM((2, 2 * nb, nz), f32),
            pltpu.VMEM((2, 8, segs), f32),
            pltpu.VMEM((nc, 8, segs), f32),
            pltpu.VMEM((n, 8, segs), f32),
            dma((len(operands),)), dma((n,)), dma((n,)), dma((n,)), dma((n,)), dma((n,)), dma((n,)), dma((2,)), dma((2,)), dma((2,)), dma((2,)),
            dma((nc,)), dma((nc,)), dma((n,)), dma((n,)),
        ],
        compiler_params=pltpu.CompilerParams(
            collective_id=0, has_side_effects=True, vmem_limit_bytes=48 * 1024 * 1024
        ),
    )(*operands)
    return grad.reshape(cotangent.shape), gain.reshape(SEG_DEV)


def solution(mesh):
    in_specs = (
        P("axial", None, "cross", None),
        P("axial", None, None),
        P("axial", None),
        P("axial", None),
        P(),
        P(),
        P(),
        P("axial", "cross"),
    )
    out_specs = (P("axial", None, "cross", None), P(("axial", "cross")))
    return jax.shard_map(
        functools.partial(per_device, mesh.shape["axial"], mesh.shape["cross"]),
        mesh=mesh, in_specs=in_specs, out_specs=out_specs, check_vma=False,
    )
```

time: 55.6 us -> 42.7 us (0.77)
  Pallas kernels: 52 us -> 40.4 us
  local copies, waits for them, and re-layouts: 2.81 us -> 1.48 us
    pallas_call x1, Pallas kernels: 52 us -> 40.4 us  [per_device(): pl.pallas_call(functools.partial(kernel, n, nc), out_shape=(pltpu.VMEM((s...]
    unnamed x4 -> x2, local copies, waits for them, and re-layouts: 2.81 us -> 1.48 us
where the time goes in v1:
time: 42.7 us; the launch traced here: 42.5 us
  Pallas kernels  40.4 us (95%)
  local copies, waits for them, and re-layouts  1.48 us (3%)
  between operations  0.64 us (1%)
    pallas_call x1, Pallas kernels, per_device(): pl.pallas_call(functools.partial(kernel, n, nc), out_shape=(pltpu.VMEM((s...  40.4 us
    unnamed x2, local copies, waits for them, and re-layouts  1.48 us

profile of v1, /device:TPU:0, one launch (start us, length us, event | category | flops | bytes accessed | tf_op | source)
XLA Modules:
  0.0 42.5 jit_solution(7211009886686405530)
XLA Ops:
  0.6 40.4 %shard_map.95 = (f32[2048,128]{1,0:T(8,128)S(1)}, f32[1,4]{1,0:T(1,128)S(1)}) custom-call(f32[2048,128]{1,0:T(8,128)} %bitcast.8, f32[16,32,32]{2,1,0:T(8,128)} %diag_hbm.1, f32[16,32]{1,0:T(8,128)} %low_hbm.1, f32[16,32]{1,0:T(8,128)} %up_hbm.1, f32[1,32]{1,0:T(1,128)} %bitcast.10, f32[1,32]{1,0:T(1,128)} %bitcast.11, s32[16,128]{1,0:T(8,128)} %open_hbm.1, ...), custom_call_target="tpu_custom_call" | custom-call | tf_op jit(solution)/shard_map/pallas_call | solution.py:444
  41.0 1.0 %copy.12 = f32[16,32,4,128]{3,2,1,0:T(4,128)} copy(f32[16,32,4,128]{3,2,1,0:T(4,128)S(1)} %bitcast.6) | data formatting | bytes 2097152
  42.0 0.5 %copy.13 = f32[4]{0:T(128)} copy(f32[4]{0:T(128)S(1)} %bitcast.7) | data formatting | bytes 32

commit v2 on v1

v2 whole, which is shorter than its diff:
```python
import functools

import jax
import jax.numpy as jnp
from jax import lax
from jax.experimental import pallas as pl
from jax.experimental.pallas import tpu as pltpu
from jax.sharding import PartitionSpec as P

SEG_DEV = 4
EARLY = 2
MESH = pl.DeviceIdType.MESH
exact = lax.Precision.HIGHEST


def dot(a, b):
    return jnp.dot(a, b, precision=exact, preferred_element_type=jnp.float32)


def halves(x):
    high = x.astype(jnp.bfloat16)
    return high, (x - high.astype(jnp.float32)).astype(jnp.bfloat16)


def dot_halves(a, b):
    (ah, al), (bh, bl) = a, b
    one = functools.partial(jnp.dot, preferred_element_type=jnp.float32)
    return one(ah, bh) + (one(ah, bl) + one(al, bh))


def dot_split(a, b):
    return dot_halves(a, halves(b))


def dot3(a, b):
    return dot_halves(halves(a), halves(b))


def dot_split_b(a, b):
    return dot_halves(halves(a), b)


def spread(x, k, nb):
    packs, height, width = x.shape
    flat = x.reshape(packs * height, width)
    lane = lax.broadcasted_iota(jnp.int32, flat.shape, 1)
    return jnp.take_along_axis(flat, lane // nb * nb + k, axis=1).reshape(x.shape)


def invert_packs(a, nb, by_two=False):
    packs, _, width = a.shape
    row_id = lax.broadcasted_iota(jnp.int32, (packs, 8, width), 1)
    for first in range(0, nb, 8):
        home = a[:, first : first + 8]
        rest = [x for x in (a[:, :first], a[:, first + 8 :]) if x.shape[1]]
        rest = jnp.concatenate(rest, axis=1) if len(rest) > 1 else rest[0]
        near = [spread(home, first + j, nb) for j in range(8)]
        far = [spread(rest, first + j, nb) for j in range(8)]
        at = lax.broadcasted_iota(jnp.int32, home.shape, 2) % nb - first
        home = jnp.where((at >= 0) & (at < 8), jnp.where(at == row_id, 1.0, 0.0), home)
        at = lax.broadcasted_iota(jnp.int32, rest.shape, 2) % nb - first
        rest = jnp.where((at >= 0) & (at < 8), 0.0, rest)
        for j in range(0, 8, 2) if by_two else ():
            pick = lambda x, i: jnp.broadcast_to(x[:, i : i + 1], home.shape)
            a00, a01, a10, a11 = pick(near[j], j), pick(near[j + 1], j), pick(near[j], j + 1), pick(near[j + 1], j + 1)
            pivot = 1.0 / (a00 * a11 - a01 * a10)
            a00, a01, a10, a11 = a11 * pivot, a01 * pivot, a10 * pivot, a00 * pivot
            first_col, second_col = near[j], near[j + 1]

            def step(x):
                x0, x1 = pick(x, j), pick(x, j + 1)
                y0, y1 = a00 * x0 - a01 * x1, a11 * x1 - a10 * x0
                done = x - (first_col * y0 + second_col * y1)
                return jnp.where(row_id == j, y0, jnp.where(row_id == j + 1, y1, done))

            home = step(home)
            for m in range(j + 2, 8):
                near[m] = step(near[m])
        for j in range(8) if not by_two else ():
            pivot = 1.0 / jnp.broadcast_to(near[j][:, j : j + 1], home.shape)
            row = jnp.broadcast_to(home[:, j : j + 1], home.shape) * pivot
            home = jnp.where(row_id == j, row, home - near[j] * row)
            for m in range(j + 1, 8):
                entry = jnp.broadcast_to(near[m][:, j : j + 1], home.shape) * pivot
                near[m] = jnp.where(row_id == j, entry, near[m] - near[j] * entry)
        for j in range(8):
            rest = rest - far[j] * home[:, j : j + 1]
        a = jnp.concatenate([x for x in (rest[:, :first], home, rest[:, first:]) if x.shape[1]], axis=1)
    return a


def invert(mats):
    nb = mats[0].shape[0]
    pack = 128 // nb
    padded = list(mats)
    while len(padded) % pack:
        padded.append(mats[len(padded) % len(mats)])
    packs = [jnp.concatenate(padded[i : i + pack], axis=1) for i in range(0, len(padded), pack)]
    done = invert_packs(jnp.stack(packs), nb, True)
    return [done[i // pack, :, i % pack * nb : (i % pack + 1) * nb] for i in range(len(mats))]


def kernel(n, nc, cot_hbm, diag_hbm, low_hbm, up_hbm, cross_hbm, prof_hbm, open_hbm, seg_hbm, out, out_seg, GH, GL, FH, FL,
           cot, diag, low, up, cross_rate, prof_rate, open_ref, seg, G, F, X, V, port_out, port_in, msg_out, msg_in, pair_out, pair_in, back_out, back_in,
           edge_in, gain_out, gain_in, s_in, s_port, r_port, s_pair, r_pair, s_msg, r_msg, s_back, r_back, s_hal, r_hal,
           s_edge, r_edge, s_gain, r_gain):
    pairs_in = [(cot_hbm, cot), (diag_hbm, diag), (low_hbm, low), (up_hbm, up), (cross_hbm, cross_rate), (prof_hbm, prof_rate),
                (open_hbm, open_ref), (seg_hbm, seg)]
    loads = [pltpu.make_async_copy(src, dst, s_in.at[i]) for i, (src, dst) in enumerate(pairs_in)]
    for i in (1, 0, 2, 3, 4, 5, 6, 7):
        loads[i].start()
    cells, nb = diag.shape[0], diag.shape[1]
    size = cells * nb
    rows = cot.shape[0] // size
    nz = cot.shape[1]
    a = lax.axis_index("axial")
    h = n // 2
    per = rows * nz // h
    is_left = a < h
    own = lax.rem(a, h)
    half_of = a - own
    partner = lax.rem(a + h, n)
    c = lax.axis_index("cross")
    has_lo = c > 0
    has_hi = c < nc - 1

    barrier = pltpu.get_barrier_semaphore()
    peers = [(i, j) for i in range(n) for j in range(nc) if i or j]
    for i, j in peers:
        pl.semaphore_signal(barrier, inc=1, device_id=(lax.rem(a + i, n), lax.rem(c + j, nc)), device_id_type=MESH)

    for i in range(2, 8):
        loads[i].wait()
    V[...] = jnp.zeros(V.shape, jnp.float32)
    V[0:cells, 0:nb] = low[...]
    V[cells : 2 * cells, 0:nb] = up[...]
    V[2 * cells : 2 * cells + 1, 0:nb] = cross_rate[...]
    V[2 * cells + 2 : 2 * cells + 2 + rows, 0:cells] = seg[...].astype(jnp.float32)
    V[...] = V[...].T
    low_col = [V[0:nb, j : j + 1] for j in range(cells)]
    up_col = [V[0:nb, cells + j : cells + j + 1] for j in range(cells)]
    cross_col = V[0:nb, 2 * cells : 2 * cells + 1]
    seg_col = [V[0:cells, 2 * cells + 2 + y : 2 * cells + 3 + y] for y in range(rows)]
    eye = (lax.broadcasted_iota(jnp.int32, (nb, nb), 0) == lax.broadcasted_iota(jnp.int32, (nb, nb), 1)).astype(jnp.float32)

    loads[1].wait()
    pack = 128 // nb
    inverses = invert_packs(
        jnp.stack([jnp.concatenate([diag[g * pack + i] for i in range(pack)], axis=1) for g in range(cells // pack)]), nb)
    tall = [inverses[g].T for g in range(cells // pack)]

    loads[0].wait()
    for y in range(rows):
        F[:, (y + 1) * nz : (y + 2) * nz] = cot[pl.ds(y, size, stride=rows), :]
    main = slice(nz, (rows + 1) * nz)

    pl.semaphore_wait(barrier, len(peers))

    def hal_copy(down):
        src = F.at[:, nz : 2 * nz] if down else F.at[:, rows * nz : (rows + 1) * nz]
        dst = F.at[:, (rows + 1) * nz : (rows + 2) * nz] if down else F.at[:, 0:nz]
        way = 0 if down else 1
        return pltpu.make_async_remote_copy(
            src_ref=src, dst_ref=dst, send_sem=s_hal.at[way], recv_sem=r_hal.at[way],
            device_id=(a, c - 1 if down else c + 1), device_id_type=MESH)

    each = h // rows
    sends_down = jnp.logical_and(has_lo, own < each)
    sends_up = jnp.logical_and(has_hi, own >= h - each)

    def edge_copy(down, off):
        way = 0 if down else 1
        slot = own if down else own - (h - each)
        peer = lax.rem(own + off, h)
        return pltpu.make_async_remote_copy(
            src_ref=back_out.at[peer], dst_ref=edge_in.at[way, slot], send_sem=s_edge.at[way, off], recv_sem=r_edge.at[way, slot],
            device_id=(half_of + peer, c - 1 if down else c + 1), device_id_type=MESH)

    def edge_wait(way):
        for e in range(each):
            pltpu.make_async_remote_copy(
                src_ref=back_out.at[e], dst_ref=edge_in.at[way, e], send_sem=s_edge.at[way, e], recv_sem=r_edge.at[way, e],
                device_id=(a, c + 1 if way == 0 else c - 1), device_id_type=MESH).wait_recv()

    @pl.when(has_lo)
    def _():
        hal_copy(True).start()

    @pl.when(has_hi)
    def _():
        hal_copy(False).start()

    @pl.when(jnp.logical_not(has_lo))
    def _():
        F[:, 0:nz] = jnp.zeros((size, nz), jnp.float32)

    @pl.when(jnp.logical_not(has_hi))
    def _():
        F[:, (rows + 1) * nz : (rows + 2) * nz] = jnp.zeros((size, nz), jnp.float32)

    FH[:, main], FL[:, main] = halves(F[:, main])

    groups = []
    for i in range(cells):
        one = tall[i // pack][i % pack * nb : (i % pack + 1) * nb]
        groups.append(jnp.concatenate([low_col[i] * one, up_col[i] * one], axis=0))
    levels = []
    while len(groups) > 1:
        pairs = [(groups[i], groups[i + 1]) for i in range(0, len(groups), 2)]
        width = groups[0].shape[1]
        none = jnp.zeros((nb, width), jnp.float32)
        meets = [dot(r[:, 0:nb], l[nb:]) for l, r in pairs]
        weights = invert([eye - k[:nb, width - nb :] for k in meets])
        level = [dot(w, jnp.concatenate([k[:nb], r[:nb]], axis=1)) for (l, r), k, w in zip(pairs, meets, weights)]
        groups = []
        for (l, r), k, p in zip(pairs, meets, level):
            base = jnp.concatenate([jnp.concatenate([l[:nb], none], axis=1), jnp.concatenate([k[nb:], r[nb:]], axis=1)], axis=0)
            groups.append(base + dot(jnp.concatenate([l[:nb, width - nb :], k[nb:, width - nb :]], axis=0), p))
        levels.append(level)

    ends = groups[0]
    ports = jnp.concatenate([ends[:, 0:nb], ends[:, size - nb : size]], axis=1)
    port_out[...] = jnp.concatenate([ports[:nb], ports[nb:]], axis=1)

    def port_copy(off):
        return pltpu.make_async_remote_copy(
            src_ref=port_out, dst_ref=port_in.at[own], send_sem=s_port.at[off], recv_sem=r_port.at[off],
            device_id=(half_of + lax.rem(own + off, h), c), device_id_type=MESH)

    def msg_copy(off):
        peer = lax.rem(own + off, h)
        return pltpu.make_async_remote_copy(
            src_ref=msg_out.at[peer], dst_ref=msg_in.at[own], send_sem=s_msg.at[off], recv_sem=r_msg.at[off],
            device_id=(half_of + peer, c), device_id_type=MESH)

    def pair_copy():
        return pltpu.make_async_remote_copy(
            src_ref=pair_out, dst_ref=pair_in, send_sem=s_pair.at[0], recv_sem=r_pair.at[0],
            device_id=(partner, c), device_id_type=MESH)

    def back_copy(off):
        peer = lax.rem(own + off, h)
        return pltpu.make_async_remote_copy(
            src_ref=back_out.at[peer], dst_ref=back_in.at[own], send_sem=s_back.at[off], recv_sem=r_back.at[off],
            device_id=(half_of + peer, c), device_id_type=MESH)

    for off in range(1, h):
        port_copy(off).start()
    port_in[own] = port_out[...]
    field = dot_split_b(ends, (FH[:, main], FL[:, main]))
    fill = [jnp.zeros((2 * nb, 128 - per), jnp.float32)] if per < 128 else []
    for e in range(h):
        msg_out[e] = jnp.concatenate([field[:, e * per : (e + 1) * per]] + fill, axis=1)
    for off in range(1, h):
        msg_copy(off).start()
    msg_in[own] = msg_out[own]

    G[...] = jnp.zeros(G.shape, jnp.float32)
    same = (lax.broadcasted_iota(jnp.int32, (128, 128), 0) // nb) == (lax.broadcasted_iota(jnp.int32, (128, 128), 1) // nb)
    for g in range(cells // pack):
        G[g * 128 : (g + 1) * 128, g * 128 : (g + 1) * 128] = jnp.where(same, jnp.concatenate([tall[g]] * pack, axis=1), 0.0)
    def grow(level):
        width = level[0].shape[1] // 2
        span = max(128, 2 * width)
        places = [(2 * i * width, (2 * i + 1) * width, 2 * i * width // span * span) for i in range(len(level))]
        lefts = []
        for (o, m, lo), p in zip(places, level):
            if span > 2 * width:
                blank = [jnp.zeros((nb, x), jnp.float32) for x in (o - lo, lo + span - o - 2 * width)]
                p = jnp.concatenate([x for x in (blank[0], p, blank[1]) if x.shape[1]], axis=1)
            lefts.append(G[o:m, lo : lo + span] + dot3(G[o:m, m - nb : m], p))
        for (o, m, lo), left in zip(places, lefts):
            G[m : m + width, lo : lo + span] += dot3(G[m : m + width, m : m + nb], up_col[m // nb - 1] * left[width - nb :])
            G[o:m, lo : lo + span] = left

    for level in levels[:EARLY]:
        grow(level)

    for off in range(1, h):
        port_copy(off).wait_recv()

    lane = lax.broadcasted_iota(jnp.int32, (1, 256), 1)
    keep_l = jnp.where((lane >= nb) & (lane < 2 * nb), 0.0, 1.0)
    keep_r = jnp.where(lane < nb, 0.0, 1.0)
    field_in = None
    groups = [(port_in[d][:, 0 : 2 * nb], port_in[d][:, 2 * nb :], None) for d in range(h)]
    blank = jnp.zeros((nb, 128 - 2 * nb), jnp.float32)
    while len(groups) > 1:
        pairs = [(groups[i], groups[i + 1]) for i in range(0, len(groups), 2)]
        meets = [dot(r[0][:, 0:nb], l[1][:, nb : 2 * nb]) for l, r in pairs]
        weights = invert([eye - k for k in meets])
        if field_in is None:
            for off in range(1, h):
                msg_copy(off).wait_recv()
            field_in = [msg_in[d] for d in range(h)]
            groups = [(jnp.concatenate([f, blank, x[:nb]], axis=1), jnp.concatenate([t, blank, x[nb:]], axis=1), None)
                      for (f, t, _), x in zip(groups, field_in)]
            pairs = [(groups[i], groups[i + 1]) for i in range(0, len(groups), 2)]
        rights = [jnp.concatenate(r[0:2] if r[2] is None else r, axis=0) for l, r in pairs]
        meets = [dot(r[:, 0:nb], l[1]) for (l, _), r in zip(pairs, rights)]
        flows = [dot(w, k[:nb] * keep_l + r[:nb] * keep_r) for r, k, w in zip(rights, meets, weights)]
        groups = []
        for (l, _), r, k, p in zip(pairs, rights, meets, flows):
            left = jnp.concatenate([l[0], l[1]] if l[2] is None else [l[0], l[2], l[1]], axis=0)
            base = jnp.concatenate([left * keep_l, k[nb:] * keep_l + r[nb:] * keep_r], axis=0)
            both = base + dot(jnp.concatenate([left[:, nb : 2 * nb], k[nb:, nb : 2 * nb]], axis=0), p)
            seam = left.shape[0]
            inner = [both[nb : seam - nb], p, both[seam - nb : seam], both[seam + nb :]]
            groups.append((both[:nb], both[seam : seam + nb], jnp.concatenate([x for x in inner if x.shape[0]], axis=0)))
    first, last, inner = groups[0]
    mine = jnp.where(is_left, last[:, nb : 2 * nb], first[:, 0:nb])
    mine_field = jnp.where(is_left, last[:, 128:], first[:, 128:])
    pair_out[0:nb] = mine_field
    pair_out[nb:] = jnp.concatenate([mine[s * nb // 4 : (s + 1) * nb // 4] for s in range(4)], axis=1)
    pair_copy().start()
    inner_port = jnp.where(is_left, inner[:, nb : 2 * nb], inner[:, 0:nb])
    inner_field = inner[:, 128:]

    for level in levels[EARLY:]:
        grow(level)
    GH[...], GL[...] = halves(G[...])

    pair_copy().wait_recv()
    theirs = jnp.concatenate([pair_in[nb:][:, s * nb : (s + 1) * nb] for s in range(4)], axis=0)
    both = dot(theirs, jnp.concatenate([mine_field, mine], axis=1))
    given = dot(invert([eye - both[:, 128:]])[0], pair_in[0:nb] + both[:, :128])
    inner = inner_field + dot(inner_port, given)
    for d in range(h):
        back_out[d, 0:nb] = inner[(2 * d - 1) * nb : 2 * d * nb] if d > 0 else jnp.where(is_left, 0.0, given)
        back_out[d, nb:] = inner[2 * d * nb : (2 * d + 1) * nb] if d < h - 1 else jnp.where(is_left, given, 0.0)
    for off in range(1, h):
        back_copy(off).start()
    back_in[own] = back_out[own]

    @pl.when(sends_down)
    def _():
        for off in range(h):
            edge_copy(True, off).start()

    @pl.when(sends_up)
    def _():
        for off in range(h):
            edge_copy(False, off).start()

    half = rows * nz // 2
    for part in range(2):
        at = slice(nz + part * half, nz + (part + 1) * half)
        X[:, at] = dot_halves((GH[...], GL[...]), (FH[:, at], FL[:, at]))

    @pl.when(has_lo)
    def _():
        hal_copy(True).wait_send()
        hal_copy(False).wait_recv()

    @pl.when(has_hi)
    def _():
        hal_copy(False).wait_send()
        hal_copy(True).wait_recv()

    sides = dot_split((GH[...], GL[...]), jnp.concatenate([F[:, 0:nz], F[:, (rows + 1) * nz : (rows + 2) * nz]], axis=1))
    X[:, 0:nz] = sides[:, 0:nz]
    X[:, (rows + 1) * nz : (rows + 2) * nz] = sides[:, nz : 2 * nz]

    sent = jnp.concatenate([prof_rate[...]] * cells, axis=1)
    mine = lax.broadcasted_iota(jnp.int32, (cells, size), 1) // nb == lax.broadcasted_iota(jnp.int32, (cells, size), 0)
    sent = dot_halves(halves(jnp.where(mine, sent, 0.0)), (GH[...], GL[...]))
    emit = dot_split_b(sent, (FH[:, main], FL[:, main]))
    sent = jnp.concatenate([sent[:, 0:nb], sent[:, size - nb : size]], axis=1)

    for off in range(1, h):
        back_copy(off).wait_recv()

    flux = []
    for y in range(rows):
        flux.append(jnp.concatenate([back_in[y * each + e][:, 0:per] for e in range(each)], axis=1))
    opens = []
    for y in range(-1, rows + 1):
        at = jnp.clip(c * rows + y, 0, nc * rows - 1)
        line = open_ref[pl.ds(at, 1), :].astype(jnp.float32)
        if y == -1:
            line = jnp.where(has_lo, line, 0.0)
        if y == rows:
            line = jnp.where(has_hi, line, 0.0)
        opens.append(line)

    segs = gain_out.shape[-1]
    seg_id = lax.broadcasted_iota(jnp.int32, (1, segs), 1)
    gain = jnp.zeros((8, segs), jnp.float32)
    flux = halves(jnp.concatenate(flux, axis=1))
    emit = emit + dot_halves(halves(sent), flux)
    for y in range(rows):
        given = jnp.sum(emit[:, y * nz : (y + 1) * nz] * opens[y + 1], axis=1, keepdims=True) * (1.0 / nz)
        picked = jnp.where(seg_col[y] == seg_id.astype(jnp.float32), given, 0.0)
        for i in range(cells // 8):
            gain = gain + picked[i * 8 : (i + 1) * 8]
    gain_out[0] = jnp.sum(gain, axis=0, keepdims=True)

    def gain_copy(k):
        i, j = peers[k]
        return pltpu.make_async_remote_copy(
            src_ref=gain_out.at[0], dst_ref=gain_in.at[k], send_sem=s_gain.at[0], recv_sem=r_gain.at[0],
            device_id=(lax.rem(a + i, n), lax.rem(c + j, nc)), device_id_type=MESH)

    for k in range(len(peers)):
        gain_copy(k).start()

    gc = (jnp.concatenate([GH[:, 0:nb], GH[:, size - nb : size]], axis=1),
          jnp.concatenate([GL[:, 0:nb], GL[:, size - nb : size]], axis=1))
    X[:, main] += dot_halves(gc, flux)

    zlane = lax.broadcasted_iota(jnp.int32, (1, nz), 1)
    step_col = jnp.concatenate([cross_col] * 4, axis=0)
    block = 4 * nb
    for y in list(range(1, rows - 1)) + [0, rows - 1]:
        if y == 0:
                @pl.when(has_lo)
                def _():
                    edge_wait(1)
                    X[:, 0:nz] += dot_split(gc, jnp.concatenate([edge_in[1, e][:, 0:per] for e in range(each)], axis=1))

                @pl.when(has_hi)
                def _():
                    edge_wait(0)
                    X[:, (rows + 1) * nz : (rows + 2) * nz] += dot_split(
                        gc, jnp.concatenate([edge_in[0, e][:, 0:per] for e in range(each)], axis=1))

        here = opens[y + 1]
        before = jnp.where(zlane == 0, 0.0, pltpu.roll(here, 1, 1)) * here
        after = jnp.where(zlane == nz - 1, 0.0, pltpu.roll(here, nz - 1, 1)) * here
        above = opens[y] * here
        below = opens[y + 2] * here
        total = before + after + above + below
        for i in range(size // block):
            at = slice(i * block, (i + 1) * block)
            x = X[at, (y + 1) * nz : (y + 2) * nz]
            moved = (above * (X[at, y * nz : (y + 1) * nz] - x) + below * (X[at, (y + 2) * nz : (y + 3) * nz] - x)
                     + before * (pltpu.roll(x, 1, 1) - x) + after * (pltpu.roll(x, nz - 1, 1) - x))
            out[pl.ds(i * block * rows + y, block, stride=rows), :] = x + step_col * moved

    pltpu.make_async_copy(gain_in, gain_in, r_gain.at[0]).wait()
    gain = gain_out[0] + jnp.sum(gain_in[...], axis=0)
    held = out_seg.shape[1]
    held_id = lax.broadcasted_iota(jnp.int32, (1, held), 1)
    result = jnp.zeros((1, held), jnp.float32)
    for j in range(held):
        picked = jnp.sum(jnp.where(seg_id == (a * nc + c) * held + j, gain, 0.0), axis=1, keepdims=True)
        result = jnp.where(held_id == j, picked, result)
    out_seg[...] = result

    pltpu.make_async_copy(gain_in, gain_in, s_gain.at[0]).wait()

    @pl.when(sends_down)
    def _():
        for off in range(h):
            edge_copy(True, off).wait_send()

    @pl.when(sends_up)
    def _():
        for off in range(h):
            edge_copy(False, off).wait_send()

    pair_copy().wait_send()
    for off in range(1, h):
        port_copy(off).wait_send()
        msg_copy(off).wait_send()
        back_copy(off).wait_send()


def per_device(n, nc, cotangent, diag_blocks, lower_rates, upper_rates, cross_rate, bin_profile, open_cells, segment_ids):
    cells, nb, rows, nz = cotangent.shape
    size, h = cells * nb, n // 2
    segs = SEG_DEV * n * nc
    vmem = pl.BlockSpec(memory_space=pltpu.VMEM)
    hbm = pl.BlockSpec(memory_space=pltpu.HBM)
    dma = pltpu.SemaphoreType.DMA
    f32 = jnp.float32
    operands = (
        cotangent.reshape(size * rows, nz), diag_blocks, lower_rates, upper_rates,
        cross_rate.reshape(1, nb), bin_profile.reshape(1, nb), open_cells, segment_ids.T,
    )
    operands = [pltpu.with_memory_space_constraint(x, pltpu.HBM) for x in operands]
    grad, gain = pl.pallas_call(
        functools.partial(kernel, n, nc),
        out_shape=(pltpu.VMEM((size * rows, nz), f32), jax.ShapeDtypeStruct((1, SEG_DEV), f32)),
        in_specs=[hbm] * len(operands),
        out_specs=(vmem, vmem),
        scratch_shapes=[pltpu.VMEM((size, size), jnp.bfloat16)] * 2 + [pltpu.VMEM((size, rows * nz + 2 * nz), jnp.bfloat16)] * 2 + [pltpu.VMEM(x.shape, x.dtype) for x in operands] + [
            pltpu.VMEM((size, size), f32),
            pltpu.VMEM((size, (rows + 2) * nz), f32),
            pltpu.VMEM((size, (rows + 2) * nz), f32),
            pltpu.VMEM((128, 128), f32),
            pltpu.VMEM((nb, 128), f32),
            pltpu.VMEM((h, nb, 128), f32),
            pltpu.VMEM((h, 2 * nb, 128), f32),
            pltpu.VMEM((h, 2 * nb, 128), f32),
            pltpu.VMEM((nb + nb // 4, 128), f32),
            pltpu.VMEM((nb + nb // 4, 128), f32),
            pltpu.VMEM((h, 2 * nb, 128), f32),
            pltpu.VMEM((h, 2 * nb, 128), f32),
            pltpu.VMEM((2, h // rows, 2 * nb, 128), f32),
            pltpu.VMEM((1, 1, segs), f32),
            pltpu.VMEM((n * nc - 1, 1, segs), f32),
            dma((len(operands),)), dma((h,)), dma((h,)), dma((1,)), dma((1,)), dma((h,)), dma((h,)), dma((h,)), dma((h,)), dma((2,)), dma((2,)), dma((2, h)), dma((2, h // rows)), dma((1,)), dma((1,)),
        ],
        compiler_params=pltpu.CompilerParams(
            collective_id=0, has_side_effects=True, vmem_limit_bytes=48 * 1024 * 1024
        ),
    )(*operands)
    return grad.reshape(cotangent.shape), gain.reshape(SEG_DEV)


def solution(mesh):
    in_specs = (
        P("axial", None, "cross", None),
        P("axial", None, None),
        P("axial", None),
        P("axial", None),
        P(),
        P(),
        P(),
        P("axial", "cross"),
    )
    out_specs = (P("axial", None, "cross", None), P(("axial", "cross")))
    return jax.shard_map(
        functools.partial(per_device, mesh.shape["axial"], mesh.shape["cross"]),
        mesh=mesh, in_specs=in_specs, out_specs=out_specs, check_vma=False,
    )
```

time: 42.7 us -> 36.8 us (0.86)
  Pallas kernels: 40.4 us -> 34.5 us
    pallas_call x1, Pallas kernels: 40.4 us -> 34.5 us  [per_device(): pl.pallas_call(functools.partial(kernel, n, nc), out_shape=(pltpu.VMEM((s...]
where the time goes in v2:
time: 36.8 us; the launch traced here: 36.6 us
  Pallas kernels  34.5 us (94%)
  local copies, waits for them, and re-layouts  1.48 us (4%)
  between operations  0.64 us (2%)
    pallas_call x1, Pallas kernels, per_device(): pl.pallas_call(functools.partial(kernel, n, nc), out_shape=(pltpu.VMEM((s...  34.5 us
    unnamed x2, local copies, waits for them, and re-layouts  1.48 us

profile of v2, /device:TPU:0, one launch (start us, length us, event | category | flops | bytes accessed | tf_op | source)
XLA Modules:
  0.0 36.6 jit_solution(15344487665334580472)
XLA Ops:
  0.6 34.5 %shard_map.95 = (f32[2048,128]{1,0:T(8,128)S(1)}, f32[1,4]{1,0:T(1,128)S(1)}) custom-call(f32[2048,128]{1,0:T(8,128)} %bitcast.8, f32[16,32,32]{2,1,0:T(8,128)} %diag_hbm.1, f32[16,32]{1,0:T(8,128)} %low_hbm.1, f32[16,32]{1,0:T(8,128)} %up_hbm.1, f32[1,32]{1,0:T(1,128)} %bitcast.10, f32[1,32]{1,0:T(1,128)} %bitcast.11, s32[16,128]{1,0:T(8,128)} %open_hbm.1, ...), custom_call_target="tpu_custom_call" | custom-call | tf_op jit(solution)/shard_map/pallas_call | solution.py:482
  35.1 1.0 %copy.12 = f32[16,32,4,128]{3,2,1,0:T(4,128)} copy(f32[16,32,4,128]{3,2,1,0:T(4,128)S(1)} %bitcast.6) | data formatting | bytes 2097152
  36.1 0.5 %copy.13 = f32[4]{0:T(128)} copy(f32[4]{0:T(128)S(1)} %bitcast.7) | data formatting | bytes 32

commit v3 on v2

--- a/solution.py
+++ b/solution.py
@@ -101,9 +101,9 @@
 
 
 def kernel(n, nc, cot_hbm, diag_hbm, low_hbm, up_hbm, cross_hbm, prof_hbm, open_hbm, seg_hbm, out, out_seg, GH, GL, FH, FL,
-           cot, diag, low, up, cross_rate, prof_rate, open_ref, seg, G, F, X, V, port_out, port_in, msg_out, msg_in, pair_out, pair_in, back_out, back_in,
+           cot, diag, low, up, cross_rate, prof_rate, open_ref, seg, G, F, X, V, port_out, port_in, msg_out, msg_in, pair_out, pair_in, back_out, back_in, mark_out, mark_in,
            edge_in, gain_out, gain_in, s_in, s_port, r_port, s_pair, r_pair, s_msg, r_msg, s_back, r_back, s_hal, r_hal,
-           s_edge, r_edge, s_gain, r_gain):
+           s_edge, r_edge, s_gain, r_gain, s_mark, r_mark):
     pairs_in = [(cot_hbm, cot), (diag_hbm, diag), (low_hbm, low), (up_hbm, up), (cross_hbm, cross_rate), (prof_hbm, prof_rate),
                 (open_hbm, open_ref), (seg_hbm, seg)]
     loads = [pltpu.make_async_copy(src, dst, s_in.at[i]) for i, (src, dst) in enumerate(pairs_in)]
@@ -233,9 +233,10 @@
             src_ref=msg_out.at[peer], dst_ref=msg_in.at[own], send_sem=s_msg.at[off], recv_sem=r_msg.at[off],
             device_id=(half_of + peer, c), device_id_type=MESH)
 
-    def pair_copy():
-        return pltpu.make_async_remote_copy(
-            src_ref=pair_out, dst_ref=pair_in, send_sem=s_pair.at[0], recv_sem=r_pair.at[0],
+    def pair_copy(which):
+        rest = pl.ds(nb, nb // 4) if which == 0 else pl.ds(0, nb)
+        return pltpu.make_async_remote_copy(
+            src_ref=pair_out.at[rest], dst_ref=pair_in.at[rest], send_sem=s_pair.at[which], recv_sem=r_pair.at[which],
             device_id=(partner, c), device_id_type=MESH)
 
     def back_copy(off):
@@ -310,69 +311,35 @@
     first, last, inner = groups[0]
     mine = jnp.where(is_left, last[:, nb : 2 * nb], first[:, 0:nb])
     mine_field = jnp.where(is_left, last[:, 128:], first[:, 128:])
+    pair_out[nb:] = jnp.concatenate([mine[s * nb // 4 : (s + 1) * nb // 4] for s in range(4)], axis=1)
+    pair_copy(0).start()
     pair_out[0:nb] = mine_field
-    pair_out[nb:] = jnp.concatenate([mine[s * nb // 4 : (s + 1) * nb // 4] for s in range(4)], axis=1)
-    pair_copy().start()
+    pair_copy(1).start()
     inner_port = jnp.where(is_left, inner[:, nb : 2 * nb], inner[:, 0:nb])
     inner_field = inner[:, 128:]
 
     for level in levels[EARLY:]:
         grow(level)
     GH[...], GL[...] = halves(G[...])
-
-    pair_copy().wait_recv()
-    theirs = jnp.concatenate([pair_in[nb:][:, s * nb : (s + 1) * nb] for s in range(4)], axis=0)
-    both = dot(theirs, jnp.concatenate([mine_field, mine], axis=1))
-    given = dot(invert([eye - both[:, 128:]])[0], pair_in[0:nb] + both[:, :128])
-    inner = inner_field + dot(inner_port, given)
-    for d in range(h):
-        back_out[d, 0:nb] = inner[(2 * d - 1) * nb : 2 * d * nb] if d > 0 else jnp.where(is_left, 0.0, given)
-        back_out[d, nb:] = inner[2 * d * nb : (2 * d + 1) * nb] if d < h - 1 else jnp.where(is_left, given, 0.0)
-    for off in range(1, h):
-        back_copy(off).start()
-    back_in[own] = back_out[own]
-
-    @pl.when(sends_down)
-    def _():
-        for off in range(h):
-            edge_copy(True, off).start()
-
-    @pl.when(sends_up)
-    def _():
-        for off in range(h):
-            edge_copy(False, off).start()
-
-    half = rows * nz // 2
-    for part in range(2):
-        at = slice(nz + part * half, nz + (part + 1) * half)
-        X[:, at] = dot_halves((GH[...], GL[...]), (FH[:, at], FL[:, at]))
-
-    @pl.when(has_lo)
-    def _():
-        hal_copy(True).wait_send()
-        hal_copy(False).wait_recv()
-
-    @pl.when(has_hi)
-    def _():
-        hal_copy(False).wait_send()
-        hal_copy(True).wait_recv()
-
-    sides = dot_split((GH[...], GL[...]), jnp.concatenate([F[:, 0:nz], F[:, (rows + 1) * nz : (rows + 2) * nz]], axis=1))
-    X[:, 0:nz] = sides[:, 0:nz]
-    X[:, (rows + 1) * nz : (rows + 2) * nz] = sides[:, nz : 2 * nz]
-
     sent = jnp.concatenate([prof_rate[...]] * cells, axis=1)
-    mine = lax.broadcasted_iota(jnp.int32, (cells, size), 1) // nb == lax.broadcasted_iota(jnp.int32, (cells, size), 0)
-    sent = dot_halves(halves(jnp.where(mine, sent, 0.0)), (GH[...], GL[...]))
-    emit = dot_split_b(sent, (FH[:, main], FL[:, main]))
+    home_cell = lax.broadcasted_iota(jnp.int32, (cells, size), 1) // nb == lax.broadcasted_iota(jnp.int32, (cells, size), 0)
+    sent = dot_halves(halves(jnp.where(home_cell, sent, 0.0)), (GH[...], GL[...]))
+    sent_all = sent
     sent = jnp.concatenate([sent[:, 0:nb], sent[:, size - nb : size]], axis=1)
-
-    for off in range(1, h):
-        back_copy(off).wait_recv()
-
-    flux = []
-    for y in range(rows):
-        flux.append(jnp.concatenate([back_in[y * each + e][:, 0:per] for e in range(each)], axis=1))
+    idle = jnp.zeros((cells, 127 - 2 * nb), jnp.float32)
+    for e in range(h):
+        mark_out[e] = jnp.concatenate([sent, seg_col[e // each], idle], axis=1)
+
+    def mark_copy(off):
+        peer = lax.rem(own + off, h)
+        return pltpu.make_async_remote_copy(
+            src_ref=mark_out.at[peer], dst_ref=mark_in.at[own], send_sem=s_mark.at[off], recv_sem=r_mark.at[off],
+            device_id=(half_of + peer, c), device_id_type=MESH)
+
+    for off in range(1, h):
+        mark_copy(off).start()
+    mark_in[own] = mark_out[own]
+    emit = dot_split_b(sent_all, (FH[:, main], FL[:, main]))
     opens = []
     for y in range(-1, rows + 1):
         at = jnp.clip(c * rows + y, 0, nc * rows - 1)
@@ -386,13 +353,48 @@
     segs = gain_out.shape[-1]
     seg_id = lax.broadcasted_iota(jnp.int32, (1, segs), 1)
     gain = jnp.zeros((8, segs), jnp.float32)
-    flux = halves(jnp.concatenate(flux, axis=1))
-    emit = emit + dot_halves(halves(sent), flux)
     for y in range(rows):
         given = jnp.sum(emit[:, y * nz : (y + 1) * nz] * opens[y + 1], axis=1, keepdims=True) * (1.0 / nz)
         picked = jnp.where(seg_col[y] == seg_id.astype(jnp.float32), given, 0.0)
         for i in range(cells // 8):
             gain = gain + picked[i * 8 : (i + 1) * 8]
+
+    pair_copy(0).wait_recv()
+    theirs = jnp.concatenate([pair_in[nb:][:, s * nb : (s + 1) * nb] for s in range(4)], axis=0)
+    both = dot(theirs, jnp.concatenate([mine_field, mine], axis=1))
+    weight = invert([eye - both[:, 128:]])[0]
+    pair_copy(1).wait_recv()
+    given = dot(weight, pair_in[0:nb] + both[:, :128])
+    inner = inner_field + dot(inner_port, given)
+    for d in range(h):
+        back_out[d, 0:nb] = inner[(2 * d - 1) * nb : 2 * d * nb] if d > 0 else jnp.where(is_left, 0.0, given)
+        back_out[d, nb:] = inner[2 * d * nb : (2 * d + 1) * nb] if d < h - 1 else jnp.where(is_left, given, 0.0)
+    for off in range(1, h):
+        back_copy(off).start()
+    back_in[own] = back_out[own]
+
+    @pl.when(sends_down)
+    def _():
+        for off in range(h):
+            edge_copy(True, off).start()
+
+    @pl.when(sends_up)
+    def _():
+        for off in range(h):
+            edge_copy(False, off).start()
+
+    line = open_ref[pl.ds(c * rows + own // each, 1), :].astype(jnp.float32)
+    wide = line[:, 0:per]
+    for q in range(1, each):
+        wide = jnp.where(lax.rem(own, each) == q, line[:, q * per : (q + 1) * per], wide)
+    for off in range(1, h):
+        mark_copy(off).wait_recv()
+    passed = [dot3(mark_in[d][:, 0 : 2 * nb], back_out[d])[:, 0:per] for d in range(h)]
+    for d in range(h):
+        given = jnp.sum(passed[d] * wide, axis=1, keepdims=True) * (1.0 / nz)
+        picked = jnp.where(mark_in[d][:, 2 * nb : 2 * nb + 1] == seg_id.astype(jnp.float32), given, 0.0)
+        for i in range(cells // 8):
+            gain = gain + picked[i * 8 : (i + 1) * 8]
     gain_out[0] = jnp.sum(gain, axis=0, keepdims=True)
 
     def gain_copy(k):
@@ -404,6 +406,33 @@
     for k in range(len(peers)):
         gain_copy(k).start()
 
+
+    half = rows * nz // 2
+    for part in range(2):
+        at = slice(nz + part * half, nz + (part + 1) * half)
+        X[:, at] = dot_halves((GH[...], GL[...]), (FH[:, at], FL[:, at]))
+
+    @pl.when(has_lo)
+    def _():
+        hal_copy(True).wait_send()
+        hal_copy(False).wait_recv()
+
+    @pl.when(has_hi)
+    def _():
+        hal_copy(False).wait_send()
+        hal_copy(True).wait_recv()
+
+    sides = dot_split((GH[...], GL[...]), jnp.concatenate([F[:, 0:nz], F[:, (rows + 1) * nz : (rows + 2) * nz]], axis=1))
+    X[:, 0:nz] = sides[:, 0:nz]
+    X[:, (rows + 1) * nz : (rows + 2) * nz] = sides[:, nz : 2 * nz]
+
+    for off in range(1, h):
+        back_copy(off).wait_recv()
+
+    flux = []
+    for y in range(rows):
+        flux.append(jnp.concatenate([back_in[y * each + e][:, 0:per] for e in range(each)], axis=1))
+    flux = halves(jnp.concatenate(flux, axis=1))
     gc = (jnp.concatenate([GH[:, 0:nb], GH[:, size - nb : size]], axis=1),
           jnp.concatenate([GL[:, 0:nb], GL[:, size - nb : size]], axis=1))
     X[:, main] += dot_halves(gc, flux)
@@ -459,9 +488,11 @@
         for off in range(h):
             edge_copy(False, off).wait_send()
 
-    pair_copy().wait_send()
+    pair_copy(0).wait_send()
+    pair_copy(1).wait_send()
     for off in range(1, h):
         port_copy(off).wait_send()
+        mark_copy(off).wait_send()
         msg_copy(off).wait_send()
         back_copy(off).wait_send()
 
@@ -497,10 +528,12 @@
             pltpu.VMEM((nb + nb // 4, 128), f32),
             pltpu.VMEM((h, 2 * nb, 128), f32),
             pltpu.VMEM((h, 2 * nb, 128), f32),
+            pltpu.VMEM((h, cells, 128), f32),
+            pltpu.VMEM((h, cells, 128), f32),
             pltpu.VMEM((2, h // rows, 2 * nb, 128), f32),
             pltpu.VMEM((1, 1, segs), f32),
             pltpu.VMEM((n * nc - 1, 1, segs), f32),
-            dma((len(operands),)), dma((h,)), dma((h,)), dma((1,)), dma((1,)), dma((h,)), dma((h,)), dma((h,)), dma((h,)), dma((2,)), dma((2,)), dma((2, h)), dma((2, h // rows)), dma((1,)), dma((1,)),
+            dma((len(operands),)), dma((h,)), dma((h,)), dma((2,)), dma((2,)), dma((h,)), dma((h,)), dma((h,)), dma((h,)), dma((2,)), dma((2,)), dma((2, h)), dma((2, h // rows)), dma((1,)), dma((1,)), dma((h,)), dma((h,)),
         ],
         compiler_params=pltpu.CompilerParams(
             collective_id=0, has_side_effects=True, vmem_limit_bytes=48 * 1024 * 1024

time: 36.8 us -> 34.6 us (0.940)
  Pallas kernels: 34.5 us -> 32.3 us
    pallas_call x1, Pallas kernels: 34.5 us -> 32.3 us  [per_device(): pl.pallas_call(functools.partial(kernel, n, nc), out_shape=(pltpu.VMEM((s...]
where the time goes in v3:
time: 34.6 us; the launch traced here: 34.4 us
  Pallas kernels  32.3 us (93%)
  local copies, waits for them, and re-layouts  1.48 us (4%)
  between operations  0.64 us (2%)
    pallas_call x1, Pallas kernels, per_device(): pl.pallas_call(functools.partial(kernel, n, nc), out_shape=(pltpu.VMEM((s...  32.3 us
    unnamed x2, local copies, waits for them, and re-layouts  1.48 us

profile of v3, /device:TPU:0, one launch (start us, length us, event | category | flops | bytes accessed | tf_op | source)
XLA Modules:
  0.0 34.4 jit_solution(2039376096151133914)
XLA Ops:
  0.6 32.3 %shard_map.95 = (f32[2048,128]{1,0:T(8,128)S(1)}, f32[1,4]{1,0:T(1,128)S(1)}) custom-call(f32[2048,128]{1,0:T(8,128)} %bitcast.8, f32[16,32,32]{2,1,0:T(8,128)} %diag_hbm.1, f32[16,32]{1,0:T(8,128)} %low_hbm.1, f32[16,32]{1,0:T(8,128)} %up_hbm.1, f32[1,32]{1,0:T(1,128)} %bitcast.10, f32[1,32]{1,0:T(1,128)} %bitcast.11, s32[16,128]{1,0:T(8,128)} %open_hbm.1, ...), custom_call_target="tpu_custom_call" | custom-call | tf_op jit(solution)/shard_map/pallas_call | solution.py:513
  33.0 1.0 %copy.12 = f32[16,32,4,128]{3,2,1,0:T(4,128)} copy(f32[16,32,4,128]{3,2,1,0:T(4,128)S(1)} %bitcast.6) | data formatting | bytes 2097152
  33.9 0.5 %copy.13 = f32[4]{0:T(128)} copy(f32[4]{0:T(128)S(1)} %bitcast.7) | data formatting | bytes 32

commit v4 on v3

--- a/solution.py
+++ b/solution.py
@@ -107,7 +107,7 @@
     pairs_in = [(cot_hbm, cot), (diag_hbm, diag), (low_hbm, low), (up_hbm, up), (cross_hbm, cross_rate), (prof_hbm, prof_rate),
                 (open_hbm, open_ref), (seg_hbm, seg)]
     loads = [pltpu.make_async_copy(src, dst, s_in.at[i]) for i, (src, dst) in enumerate(pairs_in)]
-    for i in (1, 0, 2, 3, 4, 5, 6, 7):
+    for i in (1, 2, 3, 4, 5, 6, 7, 0):
         loads[i].start()
     cells, nb = diag.shape[0], diag.shape[1]
     size = cells * nb
@@ -144,15 +144,16 @@
     eye = (lax.broadcasted_iota(jnp.int32, (nb, nb), 0) == lax.broadcasted_iota(jnp.int32, (nb, nb), 1)).astype(jnp.float32)
 
     loads[1].wait()
+    loads[0].wait()
     pack = 128 // nb
     inverses = invert_packs(
         jnp.stack([jnp.concatenate([diag[g * pack + i] for i in range(pack)], axis=1) for g in range(cells // pack)]), nb)
     tall = [inverses[g].T for g in range(cells // pack)]
 
-    loads[0].wait()
     for y in range(rows):
         F[:, (y + 1) * nz : (y + 2) * nz] = cot[pl.ds(y, size, stride=rows), :]
     main = slice(nz, (rows + 1) * nz)
+    FH[:, main], FL[:, main] = halves(F[:, main])
 
     pl.semaphore_wait(barrier, len(peers))
 
@@ -198,7 +199,6 @@
     def _():
         F[:, (rows + 1) * nz : (rows + 2) * nz] = jnp.zeros((size, nz), jnp.float32)
 
-    FH[:, main], FL[:, main] = halves(F[:, main])
 
     groups = []
     for i in range(cells):
@@ -359,6 +359,11 @@
         for i in range(cells // 8):
             gain = gain + picked[i * 8 : (i + 1) * 8]
 
+    half = rows * nz // 2
+    for part in range(2):
+        at = slice(nz + part * half, nz + (part + 1) * half)
+        X[:, at] = dot_halves((GH[...], GL[...]), (FH[:, at], FL[:, at]))
+
     pair_copy(0).wait_recv()
     theirs = jnp.concatenate([pair_in[nb:][:, s * nb : (s + 1) * nb] for s in range(4)], axis=0)
     both = dot(theirs, jnp.concatenate([mine_field, mine], axis=1))
@@ -369,19 +374,20 @@
     for d in range(h):
         back_out[d, 0:nb] = inner[(2 * d - 1) * nb : 2 * d * nb] if d > 0 else jnp.where(is_left, 0.0, given)
         back_out[d, nb:] = inner[2 * d * nb : (2 * d + 1) * nb] if d < h - 1 else jnp.where(is_left, given, 0.0)
+    @pl.when(sends_down)
+    def _():
+        for off in range(h):
+            edge_copy(True, off).start()
+
+    @pl.when(sends_up)
+    def _():
+        for off in range(h):
+            edge_copy(False, off).start()
+
     for off in range(1, h):
         back_copy(off).start()
     back_in[own] = back_out[own]
 
-    @pl.when(sends_down)
-    def _():
-        for off in range(h):
-            edge_copy(True, off).start()
-
-    @pl.when(sends_up)
-    def _():
-        for off in range(h):
-            edge_copy(False, off).start()
 
     line = open_ref[pl.ds(c * rows + own // each, 1), :].astype(jnp.float32)
     wide = line[:, 0:per]
@@ -407,11 +413,6 @@
         gain_copy(k).start()
 
 
-    half = rows * nz // 2
-    for part in range(2):
-        at = slice(nz + part * half, nz + (part + 1) * half)
-        X[:, at] = dot_halves((GH[...], GL[...]), (FH[:, at], FL[:, at]))
-
     @pl.when(has_lo)
     def _():
         hal_copy(True).wait_send()
@@ -426,16 +427,20 @@
     X[:, 0:nz] = sides[:, 0:nz]
     X[:, (rows + 1) * nz : (rows + 2) * nz] = sides[:, nz : 2 * nz]
 
+    high = [GH[:, 0:nb], GH[:, size - nb : size]]
+    reply = jnp.concatenate(high * 2 + [GL[:, 0:nb], GL[:, size - nb : size]], axis=1)
+
+    def respond(x):
+        x, small = halves(x)
+        return jnp.dot(reply, jnp.concatenate([x, small, x], axis=0), preferred_element_type=jnp.float32)
+
     for off in range(1, h):
         back_copy(off).wait_recv()
 
     flux = []
     for y in range(rows):
         flux.append(jnp.concatenate([back_in[y * each + e][:, 0:per] for e in range(each)], axis=1))
-    flux = halves(jnp.concatenate(flux, axis=1))
-    gc = (jnp.concatenate([GH[:, 0:nb], GH[:, size - nb : size]], axis=1),
-          jnp.concatenate([GL[:, 0:nb], GL[:, size - nb : size]], axis=1))
-    X[:, main] += dot_halves(gc, flux)
+    X[:, main] += respond(jnp.concatenate(flux, axis=1))
 
     zlane = lax.broadcasted_iota(jnp.int32, (1, nz), 1)
     step_col = jnp.concatenate([cross_col] * 4, axis=0)
@@ -445,13 +450,13 @@
                 @pl.when(has_lo)
                 def _():
                     edge_wait(1)
-                    X[:, 0:nz] += dot_split(gc, jnp.concatenate([edge_in[1, e][:, 0:per] for e in range(each)], axis=1))
+                    X[:, 0:nz] += respond(jnp.concatenate([edge_in[1, e][:, 0:per] for e in range(each)], axis=1))
 
                 @pl.when(has_hi)
                 def _():
                     edge_wait(0)
-                    X[:, (rows + 1) * nz : (rows + 2) * nz] += dot_split(
-                        gc, jnp.concatenate([edge_in[0, e][:, 0:per] for e in range(each)], axis=1))
+                    X[:, (rows + 1) * nz : (rows + 2) * nz] += respond(
+                        jnp.concatenate([edge_in[0, e][:, 0:per] for e in range(each)], axis=1))
 
         here = opens[y + 1]
         before = jnp.where(zlane == 0, 0.0, pltpu.roll(here, 1, 1)) * here

time: 34.6 us -> 34.4 us (level)
  no operation moved by 1% of the time
where the time goes in v4:
time: 34.4 us; the launch traced here: 34.3 us
  Pallas kernels  32.2 us (94%)
  local copies, waits for them, and re-layouts  1.48 us (4%)
  between operations  0.64 us (2%)
    pallas_call x1, Pallas kernels, per_device(): pl.pallas_call(functools.partial(kernel, n, nc), out_shape=(pltpu.VMEM((s...  32.2 us
    unnamed x2, local copies, waits for them, and re-layouts  1.48 us

profile of v4, /device:TPU:0, one launch (start us, length us, event | category | flops | bytes accessed | tf_op | source)
XLA Modules:
  0.0 34.3 jit_solution(5825189861454523864)
XLA Ops:
  0.6 32.2 %shard_map.95 = (f32[2048,128]{1,0:T(8,128)S(1)}, f32[1,4]{1,0:T(1,128)S(1)}) custom-call(f32[2048,128]{1,0:T(8,128)} %bitcast.8, f32[16,32,32]{2,1,0:T(8,128)} %diag_hbm.1, f32[16,32]{1,0:T(8,128)} %low_hbm.1, f32[16,32]{1,0:T(8,128)} %up_hbm.1, f32[1,32]{1,0:T(1,128)} %bitcast.10, f32[1,32]{1,0:T(1,128)} %bitcast.11, s32[16,128]{1,0:T(8,128)} %open_hbm.1, ...), custom_call_target="tpu_custom_call" | custom-call | tf_op jit(solution)/shard_map/pallas_call | solution.py:518
  32.8 1.0 %copy.12 = f32[16,32,4,128]{3,2,1,0:T(4,128)} copy(f32[16,32,4,128]{3,2,1,0:T(4,128)S(1)} %bitcast.6) | data formatting | bytes 2097152
  33.8 0.5 %copy.13 = f32[4]{0:T(128)} copy(f32[4]{0:T(128)S(1)} %bitcast.7) | data formatting | bytes 32
